TPU v7x, 256 devices: a whole 4x4x8 slice. The times are simulated.
256 devices in a mesh: ctx: 32 (over z, x), head: 8 (over y, core).
Axes of the slice: x: 4, y: 4, z: 8, core: 2. Of those that a mesh axis runs over, the one named last changes fastest.
Arguments:
- queries: bfloat16 [16384, 8192], P('ctx', 'head'), may hold values from -6 to 6
- keys: bfloat16 [16384, 8192], P('ctx', 'head'), may hold values from -6 to 6
- values: bfloat16 [16384, 8192], P('ctx', 'head'), may hold values from -32 to 32, as said below
- gain: bfloat16 [8192], P('head'), may hold values from 0.25 to 1.75
- cotangent: bfloat16 [16384, 8192], P('ctx', 'head'), may hold values from -6 to 6
Outputs:
- normed: bfloat16 [16384, 8192], P('ctx', 'head')
- grad_queries: bfloat16 [16384, 8192], P('ctx', 'head')
- grad_keys: bfloat16 [16384, 8192], P('ctx', 'head')
- grad_values: bfloat16 [16384, 8192], P('ctx', 'head')
Inputs may be any that keep to these rules, and one draw needn't show every extreme that they name: `values`: entries of a symmetric law, times a factor per column and a positive factor per token.
All inputs are finite; a program needn't handle non-finite values.
Results may differ from a plain program's by a relative error of at most 0.014.
Values may be sent and summed in bfloat16 or wider, within the bound.
No kernel may reach another device: no remote copies, remote signals or barrier semaphores. Data moves between devices by JAX's collectives and lax.ppermute only.
A program may use at most 128 MiB of HBM per device.

v0:
```python
import jax
import jax.numpy as jnp
from jax import lax
from jax.sharding import PartitionSpec as P

DH = 128


def prefix_2(x, axis, join, neutral, backward):
    count = lax.axis_size(axis)
    place = lax.axis_index(axis)
    ahead = count - 1 - place if backward else place
    gathered = lax.all_gather(x.astype(jnp.bfloat16), axis)
    state = jnp.zeros_like(x) + jnp.asarray(neutral, x.dtype)

    def one(lap, state):
        source = count - 1 - lap if backward else lap
        return join(state, lax.dynamic_index_in_dim(gathered, source, 0, False).astype(x.dtype))

    return lax.fori_loop(0, ahead, one, state)


def add_states(earlier, latter):
    return earlier + latter


def body(queries, keys, values, gain, cotangent):
    tok_rows = queries.shape[0]
    width = queries.shape[1]
    heads_here = width // DH
    total_width = width * lax.axis_size("head")
    q_heads = queries.reshape(tok_rows, heads_here, DH)
    k_heads = keys.reshape(tok_rows, heads_here, DH)
    v_heads = values.reshape(tok_rows, heads_here, DH)
    positions = jnp.arange(tok_rows)
    causal = (positions[:, None] >= positions[None, :])[None]
    zero_state = jnp.zeros((heads_here, DH, DH), jnp.float32)
    local_kv = jnp.einsum("thd,the->hde", k_heads, v_heads, preferred_element_type=jnp.float32)
    prefix = prefix_2(local_kv, "ctx", add_states, zero_state, False)
    state_bf = prefix.astype(jnp.bfloat16)
    scores = jnp.einsum("thd,shd->hts", q_heads, k_heads, preferred_element_type=jnp.float32)
    attn = jnp.where(causal, scores, 0.0).astype(jnp.bfloat16)
    attended = jnp.einsum("hts,shd->thd", attn, v_heads, preferred_element_type=jnp.float32)
    attended = attended + jnp.einsum(
        "thd,hde->the", q_heads, state_bf, preferred_element_type=jnp.float32
    )
    attended = attended.reshape(tok_rows, width)
    gain_f = gain.astype(jnp.float32)
    scaled = cotangent.astype(jnp.float32) * gain_f
    square_sum, cross_sum = lax.psum(
        (jnp.sum(attended * attended, axis=1), jnp.sum(scaled * attended, axis=1)), "head"
    )
    inv_rms = lax.rsqrt(square_sum / total_width + 1e-06)
    cross = cross_sum / total_width
    normed = (attended * inv_rms[:, None] * gain_f).astype(jnp.bfloat16)
    grad_att = (inv_rms[:, None] * scaled - attended * (inv_rms**3 * cross)[:, None]).astype(
        jnp.bfloat16
    )
    g_heads = grad_att.reshape(tok_rows, heads_here, DH)
    local_grad = jnp.einsum("thd,the->hde", q_heads, g_heads, preferred_element_type=jnp.float32)
    later = prefix_2(local_grad, "ctx", add_states, zero_state, True)
    later_bf = later.astype(jnp.bfloat16)
    grad_scores = jnp.einsum("thd,shd->hts", g_heads, v_heads, preferred_element_type=jnp.float32)
    grad_attn = jnp.where(causal, grad_scores, 0.0).astype(jnp.bfloat16)
    grad_q = jnp.einsum("hts,shd->thd", grad_attn, k_heads, preferred_element_type=jnp.float32)
    grad_q = grad_q + jnp.einsum(
        "the,hde->thd", g_heads, state_bf, preferred_element_type=jnp.float32
    )
    grad_k = jnp.einsum("hts,thd->shd", grad_attn, q_heads, preferred_element_type=jnp.float32)
    grad_k = grad_k + jnp.einsum(
        "the,hde->thd", v_heads, later_bf, preferred_element_type=jnp.float32
    )
    grad_v = jnp.einsum("hts,thd->shd", attn, g_heads, preferred_element_type=jnp.float32)
    grad_v = grad_v + jnp.einsum(
        "thd,hde->the", k_heads, later_bf, preferred_element_type=jnp.float32
    )
    return (
        normed,
        grad_q.reshape(tok_rows, width).astype(jnp.bfloat16),
        grad_k.reshape(tok_rows, width).astype(jnp.bfloat16),
        grad_v.reshape(tok_rows, width).astype(jnp.bfloat16),
    )


def solution(mesh):
    return jax.shard_map(
        body,
        mesh=mesh,
        in_specs=(
            P("ctx", "head"),
            P("ctx", "head"),
            P("ctx", "head"),
            P("head"),
            P("ctx", "head"),
        ),
        out_specs=(P("ctx", "head"), P("ctx", "head"), P("ctx", "head"), P("ctx", "head")),
        check_vma=False,
    )
```

profile of v0, /device:TPU:2, one launch (start us, length us, event | category | flops | bytes accessed | tf_op | source)
XLA Modules:
  0.0 319.1 jit_solution(16139830200374923082)
XLA Ops:
  7.2 2.6 copy.65
  9.9 1.6 copy.37
  11.5 1.2 convolution_convert_fusion.1
  12.7 0.0 all-gather.7.cloned.1.call-start
  12.8 0.1 iota_compare_fusion
  12.9 2.5 select_convert_fusion.1
  15.4 1.9 copy-done.1
  17.3 2.9 fusion.3
  20.2 92.6 %all-gather.5.cloned.1.call-done = bf16[256,128,128]{2,1,0:T(8,128)(2,1)} async-done(((bf16[8,128,128]{2,1,0:T(8,128)(2,1)}), bf16[256,128,128]{2,1,0:T(8,128)(2,1)}) %all-gather.5.cloned.1.call-update) | async-done | bytes 8388624 | tf_op jit(solution)/shard_map/all_gather | solution.py:13
  112.9 1.1 while.22
  112.9 1.1 convert_add_fusion.4
  114.0 3.5 %multiply_reduce_fusion.1 = (f32[512]{0:T(512)S(1)}, f32[512,8,128]{0,2,1:T(8,128)}) fusion(f32[8,128,128]{2,1,0:T(8,128)S(1)} %get-tuple-element.83, f32[8,512,128]{1,2,0:T(8,128)} %fusion.3, bf16[512,1024]{1,0:T(8,128)(2,1)S(1)} %copy-done), kind=kOutput, calls=%fused_computation.14 | convolution fusion | flops 135921152 | bytes 5769216 | tf_op jit(solution)/shard_map/thd,hde->the/dot_general | solution.py:44
  117.5 3.0 copy.41
  120.5 1.9 multiply_reduce_fusion
  122.5 14.2 %all-reduce = (f32[512]{0:T(512)S(1)}, f32[512]{0:T(512)S(1)}) all-reduce(f32[512]{0:T(512)S(1)} %get-tuple-element.119, f32[512]{0:T(512)S(1)} %multiply_reduce_fusion), channel_id=1, replica_groups=mesh['ctx'=32,'head'=8] {'head'}, use_global_device_ids=true, to_apply=%region_3.4 | all-reduce | flops 1024 | bytes 8192 | tf_op jit(solution)/shard_map/psum | solution.py:50
  136.7 3.5 %subtract_convert_fusion = (bf16[512,1024]{1,0:T(8,128)(2,1)}, bf16[512,1024]{1,0:T(8,128)(2,1)}) fusion(f32[512,1024]{1,0:T(8,128)} %copy.41, bf16[512,1024]{1,0:T(8,128)(2,1)S(1)} %copy-done.7, f32[512]{0:T(512)S(1)} %get-tuple-element.117, f32[1024]{0:T(1024)S(1)} %convert_element_type.72, f32[512]{0:T(512)S(1)} %get-tuple-element.118), kind=kLoop, calls=%fused_computation.10 | loop fusion | flops 4718592 | bytes 5251072 | tf_op jit(solution)/shard_map/convert_element_type | solution.py:56
  140.2 1.5 copy.61
  141.7 0.5 fusion.2
  142.1 0.9 copy.51
  143.0 2.7 select_convert_fusion
  145.8 1.5 fusion.30
  147.2 0.5 copy-done.2
  147.7 1.4 fusion.1
  149.1 2.3 copy.56
  151.4 4.2 %fusion.31 = f32[8,128,512]{2,1,0:T(8,128)} fusion(bf16[512,8,128]{0,2,1:T(8,128)(2,1)S(1)} %bitcast.110, bf16[8,512,512]{2,1,0:T(8,128)(2,1)} %copy-done.1), kind=kOutput, calls=%fused_computation.49 | convolution fusion | flops 536870912 | bytes 7340032 | tf_op jit(solution)/shard_map/hts,thd->shd/dot_general | solution.py:73
  155.6 110.9 %all-gather.7.cloned.1.call-done = bf16[256,128,128]{2,1,0:T(8,128)(2,1)} async-done(((bf16[8,128,128]{2,1,0:T(8,128)(2,1)}), bf16[256,128,128]{2,1,0:T(8,128)(2,1)}) %all-gather.7.cloned.1.call-update) | async-done | bytes 8388624 | tf_op jit(solution)/shard_map/all_gather | solution.py:13
  266.6 32.9 %while.23 = (s32[]{:T(128)}, f32[8,128,128]{2,1,0:T(8,128)S(1)}, s32[]{:T(128)}, bf16[32,8,128,128]{3,2,1,0:T(8,128)(2,1)}, s32[]{:T(128)}, /*index=5*/s32[]{:T(128)}, s32[]{:T(128)}, s32[]{:T(128)}) while((s32[]{:T(128)}, f32[8,128,128]{2,1,0:T(8,128)S(1)}, s32[]{:T(128)}, bf16[32,8,128,128]{3,2,1,0:T(8,128)(2,1)}, s32[]{:T(128)}, ...), condition=%wide.region_7.8_spmd, body=%wide.region_6.7_spmd.sunk | while | flops 262150 | bytes 1310863 | solution.py:20
  266.7 1.2 convert_add_fusion.5
  267.8 1.1 convert_add_fusion.5
  268.9 1.1 convert_add_fusion.5
  270.0 1.1 convert_add_fusion.5
  271.1 1.1 convert_add_fusion.5
  272.2 1.1 convert_add_fusion.5
  273.3 1.1 convert_add_fusion.5
  274.4 1.1 convert_add_fusion.5
  275.5 1.1 convert_add_fusion.5
  276.6 1.1 convert_add_fusion.5
  277.7 1.1 convert_add_fusion.5
  278.7 1.1 convert_add_fusion.5
  279.8 1.1 convert_add_fusion.5
  280.9 1.1 convert_add_fusion.5
  282.0 1.1 convert_add_fusion.5
  283.1 1.1 convert_add_fusion.5
  284.2 1.1 convert_add_fusion.5
  285.3 1.1 convert_add_fusion.5
  286.4 1.1 convert_add_fusion.5
  287.5 1.1 convert_add_fusion.5
  288.6 1.1 convert_add_fusion.5
  289.7 1.1 convert_add_fusion.5
  290.8 1.1 convert_add_fusion.5
  291.9 1.1 convert_add_fusion.5
  292.9 1.1 convert_add_fusion.5
  294.0 1.1 convert_add_fusion.5
  295.1 1.1 convert_add_fusion.5
  296.2 1.1 convert_add_fusion.5
  297.3 1.1 convert_add_fusion.5
  298.4 1.1 convert_add_fusion.5
  299.5 1.8 fusion.5
  301.3 0.1 copy-done.3
  301.4 0.7 copy-done.10
  302.1 1.5 add_convert_fusion
  303.6 2.4 copy.58
  306.0 4.0 %fusion = bf16[512,8,128]{0,2,1:T(8,128)(2,1)} fusion(f32[8,128,512]{2,1,0:T(8,128)S(1)} %copy-done.4, bf16[8,512,512]{2,1,0:T(8,128)(2,1)} %copy-done.2, bf16[512,1024]{1,0:T(8,128)(2,1)S(1)} %copy-done), kind=kOutput, calls=%fused_computation.5 | convolution fusion | flops 537919488 | bytes 8388608 | tf_op jit(solution)/shard_map/hts,thd->shd/dot_general | solution.py:69
  310.0 2.3 copy.57
  (27 shorter events, 0.2 us)
Async XLA Ops:
  7.2 5.7 %copy-start = (bf16[512,1024]{1,0:T(8,128)(2,1)S(1)}, bf16[512,1024]{1,0:T(8,128)(2,1)}, u32[]{:S(2)}) copy-start(bf16[512,1024]{1,0:T(8,128)(2,1)} %param.9) | copy-start | bytes 3145732
  7.2 105.7 %all-gather.5.cloned.1.call-start = ((), (), s32[]{:S(2)}) async-start(), calls=%async_computation | async-start | bytes 8650752 | tf_op jit(solution)/shard_map/all_gather | solution.py:13
  7.2 4.3 %copy-start.5 = (bf16[512,1024]{1,0:T(8,128)(2,1)S(1)}, bf16[512,1024]{1,0:T(8,128)(2,1)}, u32[]{:S(2)}) copy-start(bf16[512,1024]{1,0:T(8,128)(2,1)} %param.11) | copy-start | bytes 3145732
  9.8 2.9 copy-start.11
  11.5 3.9 %copy-start.8 = (bf16[512,8,128]{0,2,1:T(8,128)(2,1)}, bf16[512,8,128]{0,2,1:T(8,128)(2,1)S(1)}, u32[]{:S(2)}) copy-start(bf16[512,8,128]{0,2,1:T(8,128)(2,1)S(1)} %copy.37) | copy-start | bytes 3145732
  12.7 253.9 %all-gather.7.cloned.1.call-start = ((), (), s32[]{:S(2)}) async-start(), calls=%async_computation.1 | async-start | bytes 8650752 | tf_op jit(solution)/shard_map/all_gather | solution.py:13
  15.4 1.9 copy-start.1
  117.5 3.0 copy-start.7
  143.0 2.7 copy-start.9
  145.8 2.0 copy-start.2
  266.6 32.9 %copy-start.6 = (bf16[512,1024]{1,0:T(8,128)(2,1)S(1)}, bf16[512,1024]{1,0:T(8,128)(2,1)}, u32[]{:S(2)}) copy-start(bf16[512,1024]{1,0:T(8,128)(2,1)} %param.11) | copy-start | bytes 3145732
  299.5 1.9 copy-start.3
  299.5 2.6 copy-start.10
  303.6 2.4 copy-start.4
Sparse Core Ops, SparseCore 0:
  12.8 100.0 all-gather.4
  143.1 123.3 all-gather.6
where the time goes:
time: 323 us; the launch traced here: 319 us
  waiting for transfers between devices  204 us (63%)
  other arithmetic  38.8 us (12%)
  matrix products  27.6 us (9%)
  local copies, waits for them, and re-layouts  19.8 us (6%)
  between operations  14.3 us (4%)
  blocking collectives  14.2 us (4%)
    all_gather x2, waiting for transfers between devices, prefix_2(): gathered = lax.all_gather(x.astype(jnp.bfloat16), axis)  204 us
    add x31, other arithmetic, add_states(): return earlier + latter  33.2 us
    psum x1, blocking collectives, body(): lax.psum((jnp.sum(attended * attended, axis=1), jnp.sum(scaled * attended...  14.2 us
    unnamed x28, local copies, waits for them, and re-layouts  12.8 us
  transfers between devices with their start and end apart: 2, of which 2 were waited for; matrix products, arithmetic and copies ran while one was open for 6% of the time, Pallas kernels for 0%

commit v1 on v0

v1 whole, which is shorter than its diff:
```python
import functools

import jax
import jax.numpy as jnp
from jax import lax
from jax.experimental import pallas as pl
from jax.experimental.pallas import tpu as pltpu
from jax.sharding import PartitionSpec as P

DH = 128
F32 = jnp.float32
BF16 = jnp.bfloat16
VMEM_LIMIT = 48 * 1024 * 1024

NT = (((1,), (1,)), ((), ()))
NN = (((1,), (0,)), ((), ()))
TN = (((0,), (0,)), ((), ()))


def dot(a, b, dims):
    return lax.dot_general(a, b, dims, preferred_element_type=F32)


def params(*axes):
    return pltpu.CompilerParams(dimension_semantics=axes, vmem_limit_bytes=VMEM_LIMIT)


def outer_kernel(a_ref, b_ref, out_ref):
    for h in range(a_ref.shape[1] // DH):
        cols = slice(h * DH, (h + 1) * DH)
        out_ref[cols, :] = dot(a_ref[:, cols], b_ref[:, cols], TN).astype(BF16)


def outer(a, b, step):
    rows, width = a.shape
    spec = pl.BlockSpec((rows, step), lambda i: (0, i))
    return pl.pallas_call(
        outer_kernel,
        grid=(width // step,),
        in_specs=[spec, spec],
        out_specs=pl.BlockSpec((step, DH), lambda i: (i, 0)),
        out_shape=jax.ShapeDtypeStruct((width, DH), BF16),
        compiler_params=params("arbitrary"),
        name="outer",
    )(a, b)


def scan_kernel(x_ref, out_ref, *, backward):
    count = x_ref.shape[0]
    total = jnp.zeros(x_ref.shape[1:], F32)
    for lap in range(count):
        i = count - 1 - lap if backward else lap
        out_ref[i] = total.astype(BF16)
        total = total + x_ref[i].astype(F32)


def scan(x, backward):
    return pl.pallas_call(
        functools.partial(scan_kernel, backward=backward),
        out_shape=jax.ShapeDtypeStruct(x.shape, BF16),
        compiler_params=params(),
        name="suffix" if backward else "prefix",
    )(x)


def exchange(x, axis):
    return lax.all_to_all(x, axis, 0, 0)


def running(local, backward):
    count = lax.axis_size("ctx")
    parts = local.reshape(count, local.shape[0] // count, DH)
    mine = scan(exchange(parts, "ctx"), backward)
    return exchange(mine, "ctx").reshape(local.shape)


def keep_lower(x):
    row = lax.broadcasted_iota(jnp.int32, x.shape, 0)
    col = lax.broadcasted_iota(jnp.int32, x.shape, 1)
    return jnp.where(row >= col, x, 0.0)


def keep_upper(x):
    row = lax.broadcasted_iota(jnp.int32, x.shape, 0)
    col = lax.broadcasted_iota(jnp.int32, x.shape, 1)
    return jnp.where(row <= col, x, 0.0)


def lower_product(a, b, c):
    half = a.shape[0] // 2
    top = keep_lower(dot(a[:half], b[:half], NT)).astype(BF16)
    low = dot(a[half:], b[:half], NT).astype(BF16)
    last = keep_lower(dot(a[half:], b[half:], NT)).astype(BF16)
    return dot(top, c[:half], NN), dot(low, c[:half], NN) + dot(last, c[half:], NN)


def upper_product(a, b, c):
    half = a.shape[0] // 2
    top = keep_upper(dot(a[:half], b[:half], NT)).astype(BF16)
    high = dot(a[:half], b[half:], NT).astype(BF16)
    last = keep_upper(dot(a[half:], b[half:], NT)).astype(BF16)
    return dot(top, c[:half], NN) + dot(high, c[half:], NN), dot(last, c[half:], NN)


def within_kernel(q_ref, k_ref, v_ref, out_ref):
    half = q_ref.shape[0] // 2
    one, two = lower_product(q_ref[...], k_ref[...], v_ref[...])
    out_ref[:half] = one
    out_ref[half:] = two


def within(q, k, v):
    rows, width = q.shape
    spec = pl.BlockSpec((rows, DH), lambda i: (0, i))
    return pl.pallas_call(
        within_kernel,
        grid=(width // DH,),
        in_specs=[spec] * 3,
        out_specs=spec,
        out_shape=jax.ShapeDtypeStruct((rows, width), F32),
        compiler_params=params("arbitrary"),
        name="within",
    )(q, k, v)


def attend_kernel(a_ref, q_ref, s_ref, cot_ref, gain_ref, att_ref, stat_ref, sq_ref, cr_ref):
    step = pl.program_id(0)

    @pl.when(step == 0)
    def _():
        sq_ref[...] = jnp.zeros_like(sq_ref)
        cr_ref[...] = jnp.zeros_like(cr_ref)

    for h in range(q_ref.shape[1] // DH):
        cols = slice(h * DH, (h + 1) * DH)
        att = a_ref[:, cols] + dot(q_ref[:, cols], s_ref[cols, :], NN)
        att_ref[:, cols] = att
        scaled = cot_ref[:, cols].astype(F32) * gain_ref[:, cols].astype(F32)
        sq_ref[...] += att * att
        cr_ref[...] += scaled * att

    @pl.when(step == pl.num_programs(0) - 1)
    def _():
        blocks = sq_ref.shape[0] // DH
        for i in range(blocks):
            rows = slice(i * DH, (i + 1) * DH)
            for j, ref in enumerate((sq_ref, cr_ref)):
                line = jnp.sum(ref[rows, :].T, axis=0, keepdims=True)
                for copy in range(stat_ref.shape[0]):
                    stat_ref[copy, j * blocks + i : j * blocks + i + 1, :] = line


def attend(a, q, s, cot, gain, copies, step):
    rows, width = q.shape
    lines = 2 * rows // DH
    spec = pl.BlockSpec((rows, step), lambda i: (0, i))
    return pl.pallas_call(
        attend_kernel,
        grid=(width // step,),
        in_specs=[
            spec,
            spec,
            pl.BlockSpec((step, DH), lambda i: (i, 0)),
            spec,
            pl.BlockSpec((1, step), lambda i: (0, i)),
        ],
        out_specs=[spec, pl.BlockSpec((copies, lines, DH), lambda i: (0, 0, 0))],
        out_shape=[
            jax.ShapeDtypeStruct((rows, width), F32),
            jax.ShapeDtypeStruct((copies, lines, DH), F32),
        ],
        scratch_shapes=[pltpu.VMEM((rows, DH), F32), pltpu.VMEM((rows, DH), F32)],
        compiler_params=params("arbitrary"),
        name="attend",
    )(a, q, s, cot, gain)


def grad_kernel(att_ref, cot_ref, gain_ref, stat_ref, q_ref, g_ref, lg_ref, rms_ref, r_ref, c_ref, *, total):
    rows = att_ref.shape[0]

    @pl.when(pl.program_id(0) == 0)
    def _():
        blocks = rows // DH
        stats = jnp.sum(stat_ref[...], axis=0) / total
        for i in range(blocks):
            span = slice(i * DH, (i + 1) * DH)
            inv = lax.rsqrt(stats[i : i + 1, :] + 1e-06)
            cross = stats[blocks + i : blocks + i + 1, :]
            inv_tile = jnp.broadcast_to(inv, (DH, DH)).T
            r_ref[span, :] = inv_tile
            rms_ref[span, :] = inv_tile
            c_ref[span, :] = jnp.broadcast_to(inv**3 * cross, (DH, DH)).T

    for h in range(q_ref.shape[1] // DH):
        cols = slice(h * DH, (h + 1) * DH)
        scaled = cot_ref[:, cols].astype(F32) * gain_ref[:, cols].astype(F32)
        g = (r_ref[...] * scaled - att_ref[:, cols] * c_ref[...]).astype(BF16)
        g_ref[:, cols] = g
        lg_ref[cols, :] = dot(q_ref[:, cols], g, TN).astype(BF16)


def grad(att, cot, gain, stats, q, total, step):
    rows, width = q.shape
    spec = pl.BlockSpec((rows, step), lambda i: (0, i))
    return pl.pallas_call(
        functools.partial(grad_kernel, total=total),
        grid=(width // step,),
        in_specs=[
            spec,
            spec,
            pl.BlockSpec((1, step), lambda i: (0, i)),
            pl.BlockSpec(stats.shape, lambda i: (0, 0, 0)),
            spec,
        ],
        out_specs=[spec, pl.BlockSpec((step, DH), lambda i: (i, 0)), pl.BlockSpec((rows, DH), lambda i: (0, 0))],
        out_shape=[
            jax.ShapeDtypeStruct((rows, width), BF16),
            jax.ShapeDtypeStruct((width, DH), BF16),
            jax.ShapeDtypeStruct((rows, DH), F32),
        ],
        scratch_shapes=[pltpu.VMEM((rows, DH), F32), pltpu.VMEM((rows, DH), F32)],
        compiler_params=params("arbitrary"),
        name="grad",
    )(att, cot, gain, stats, q)


def side_kernel(q_ref, k_ref, v_ref, g_ref, s_ref, att_ref, gain_ref, rms_ref, n_ref, gq_ref, gk_ref, gv_ref):
    half = q_ref.shape[0] // 2
    q, k, v, g = q_ref[...], k_ref[...], v_ref[...], g_ref[...]
    n_ref[...] = (att_ref[...] * rms_ref[...] * gain_ref[...].astype(F32)).astype(BF16)
    one, two = lower_product(g, v, k)
    far = dot(g, s_ref[...], NT)
    gq_ref[:half] = (one + far[:half]).astype(BF16)
    gq_ref[half:] = (two + far[half:]).astype(BF16)
    one, two = upper_product(v, g, q)
    gk_ref[:half] = one
    gk_ref[half:] = two
    one, two = upper_product(k, q, g)
    gv_ref[:half] = one
    gv_ref[half:] = two


def side(q, k, v, g, s, att, gain, rms):
    rows, width = q.shape
    spec = pl.BlockSpec((rows, DH), lambda i: (0, i))
    return pl.pallas_call(
        side_kernel,
        grid=(width // DH,),
        in_specs=[
            spec,
            spec,
            spec,
            spec,
            pl.BlockSpec((DH, DH), lambda i: (i, 0)),
            spec,
            pl.BlockSpec((1, DH), lambda i: (0, i)),
            pl.BlockSpec((rows, DH), lambda i: (0, 0)),
        ],
        out_specs=[spec] * 4,
        out_shape=[
            jax.ShapeDtypeStruct((rows, width), BF16),
            jax.ShapeDtypeStruct((rows, width), BF16),
            jax.ShapeDtypeStruct((rows, width), F32),
            jax.ShapeDtypeStruct((rows, width), F32),
        ],
        compiler_params=params("arbitrary"),
        name="side",
    )(q, k, v, g, s, att, gain, rms)


def last_kernel(gk_ref, gv_ref, k_ref, v_ref, s_ref, outk_ref, outv_ref):
    for h in range(k_ref.shape[1] // DH):
        cols = slice(h * DH, (h + 1) * DH)
        s = s_ref[cols, :]
        outk_ref[:, cols] = (gk_ref[:, cols] + dot(v_ref[:, cols], s, NT)).astype(BF16)
        outv_ref[:, cols] = (gv_ref[:, cols] + dot(k_ref[:, cols], s, NN)).astype(BF16)


def last(gk, gv, k, v, s, step):
    rows, width = k.shape
    spec = pl.BlockSpec((rows, step), lambda i: (0, i))
    return pl.pallas_call(
        last_kernel,
        grid=(width // step,),
        in_specs=[spec] * 4 + [pl.BlockSpec((step, DH), lambda i: (i, 0))],
        out_specs=[spec] * 2,
        out_shape=[jax.ShapeDtypeStruct((rows, width), BF16)] * 2,
        compiler_params=params("arbitrary"),
        name="last",
    )(gk, gv, k, v, s)


def body(queries, keys, values, gain, cotangent):
    rows, width = queries.shape
    heads = lax.axis_size("head")
    gain = gain.reshape(1, width)
    state = running(outer(keys, values, 256), False)
    a = within(queries, keys, values)
    att, stats = attend(a, queries, state, cotangent, gain, heads, 256)
    stats = exchange(stats, "head")
    g, local_grad, rms = grad(att, cotangent, gain, stats, queries, width * heads, 256)
    later = running(local_grad, True)
    normed, grad_q, gk, gv = side(queries, keys, values, g, state, att, gain, rms)
    grad_k, grad_v = last(gk, gv, keys, values, later, 256)
    return normed, grad_q, grad_k, grad_v


def solution(mesh):
    return jax.shard_map(
        body,
        mesh=mesh,
        in_specs=(
            P("ctx", "head"),
            P("ctx", "head"),
            P("ctx", "head"),
            P("head"),
            P("ctx", "head"),
        ),
        out_specs=(P("ctx", "head"), P("ctx", "head"), P("ctx", "head"), P("ctx", "head")),
        check_vma=False,
    )
```

time: 323 us -> 105 us (0.33)
  waiting for transfers between devices: 204 us -> 4.55 us
  other arithmetic: 38.8 us -> 0 us
  blocking collectives: 14.2 us -> 48.8 us
  matrix products: 27.6 us -> 0 us
  Pallas kernels: 0 us -> 26.6 us
  between operations: 14.3 us -> 0.81 us
  starting transfers between devices: 0.08 us -> 11.4 us
  local copies, waits for them, and re-layouts: 19.8 us -> 11.9 us
    all_gather x2 -> x0, waiting for transfers between devices: 204 us -> none  [prefix_2(): gathered = lax.all_gather(x.astype(jnp.bfloat16), axis)]
    all_to_all x0 -> x3, blocking collectives: none -> 48.8 us  [exchange(): return lax.all_to_all(x, axis, 0, 0)]
    add x31 -> x0, other arithmetic: 33.2 us -> none  [add_states(): return earlier + latter]
    dot_general x12 -> x0, matrix products: 27.6 us -> none  [the longest x1 4.23 us: body(): jnp.einsum('hts,thd->shd', attn, g_heads, preferred_element_type=jnp.floa...]
    pallas_call x0 -> x8, Pallas kernels: none -> 26.6 us  [the longest x1 10.8 us: side(): pl.pallas_call(side_kernel, grid=(width // DH,), in_specs=[spec, spec, sp...]
    psum x1 -> x0, blocking collectives: 14.2 us -> none  [body(): lax.psum((jnp.sum(attended * attended, axis=1), jnp.sum(scaled * attended...]
    all_to_all x0 -> x2, starting transfers between devices: none -> 11.4 us  [exchange(): return lax.all_to_all(x, axis, 0, 0)]
    reshape x3 -> x1, local copies, waits for them, and re-layouts: 6.13 us -> 0.01 us  [body(): gain = gain.reshape(1, width)]
  transfers between devices with their start and end apart: 2 -> 2, of which waited for: 2 -> 1; matrix products, arithmetic and copies ran while one was open for 6% -> 0% of each run, Pallas kernels for 0% -> 15%
where the time goes in v1:
time: 105 us; the launch traced here: 104 us
  blocking collectives  48.8 us (46%)
  Pallas kernels  26.6 us (25%)
  local copies, waits for them, and re-layouts  11.9 us (11%)
  starting transfers between devices  11.4 us (11%)
  waiting for transfers between devices  4.55 us (4%)
    all_to_all x3, blocking collectives, exchange(): return lax.all_to_all(x, axis, 0, 0)  48.8 us
    unnamed x32, local copies, waits for them, and re-layouts  11.9 us
    all_to_all x2, starting transfers between devices, exchange(): return lax.all_to_all(x, axis, 0, 0)  11.4 us
    pallas_call x1, Pallas kernels, side(): pl.pallas_call(side_kernel, grid=(width // DH,), in_specs=[spec, spec, sp...  10.8 us
    all_to_all x2, waiting for transfers between devices, exchange(): return lax.all_to_all(x, axis, 0, 0)  4.55 us
    pallas_call x1, Pallas kernels, within(): pl.pallas_call(within_kernel, grid=(width // DH,), in_specs=[spec] * 3, o...  4.45 us
    pallas_call x1, Pallas kernels, last(): pl.pallas_call(last_kernel, grid=(width // step,), in_specs=[spec] * 4 +...  4.34 us
    pallas_call x1, Pallas kernels, attend(): pl.pallas_call(attend_kernel, grid=(width // step,), in_specs=[spec, spec...  3.34 us
  transfers between devices with their start and end apart: 2, of which 1 were waited for; matrix products, arithmetic and copies ran while one was open for 0% of the time, Pallas kernels for 15%

profile of v1, /device:TPU:2, one launch (start us, length us, event | category | flops | bytes accessed | tf_op | source)
XLA Modules:
  0.0 104.1 jit_solution(16404182839694107103)
XLA Ops:
  0.6 0.0 copy-start
  0.6 0.0 copy-start.1
  0.7 1.3 %copy-done.1 = bf16[512,1024]{1,0:T(8,128)(2,1)S(1)} copy-done((bf16[512,1024]{1,0:T(8,128)(2,1)S(1)}, bf16[512,1024]{1,0:T(8,128)(2,1)}, u32[]{:S(2)}) %copy-start.1) | copy-done | bytes 1048600
  2.0 0.0 copy-start.3
  2.0 1.2 %copy-done.3 = bf16[512,1024]{1,0:T(8,128)(2,1)S(1)} copy-done((bf16[512,1024]{1,0:T(8,128)(2,1)S(1)}, bf16[512,1024]{1,0:T(8,128)(2,1)}, u32[]{:S(2)}) %copy-start.3) | copy-done | bytes 1048600
  3.2 0.0 copy-start.15
  3.2 0.0 copy-start.2
  3.2 0.0 copy-start.4
  3.2 1.4 %outer.1 = bf16[1024,128]{1,0:T(8,128)(2,1)S(1)} custom-call(bf16[512,1024]{1,0:T(8,128)(2,1)S(1)} %copy-done.1, bf16[512,1024]{1,0:T(8,128)(2,1)S(1)} %copy-done.3), custom_call_target="tpu_custom_call" | custom-call | tf_op jit(solution)/shard_map/outer/pallas_call | solution.py:37
  4.6 22.6 %all_to_all.25.x_ref = bf16[32,32,128]{2,1,0:T(8,128)(2,1)S(1)} all-to-all(bf16[32,32,128]{2,1,0:T(8,128)(2,1)S(1)} %bitcast.6), channel_id=1, replica_groups=mesh['ctx'=32,'head'=8] {'ctx'}, dimensions={0} | all-to-all | bytes 524288 | tf_op jit(solution)/shard_map/all_to_all | solution.py:67
  27.3 0.0 copy-start.10
  27.3 0.7 copy-done.10
  28.0 5.6 %all-to-all-start.1 = ((bf16[32,32,128]{2,1,0:T(8,128)(2,1)}), bf16[32,32,128]{2,1,0:T(8,128)(2,1)S(1)}, u32[]{:S(2)}, u32[]{:S(2)}) async-start(bf16[32,32,128]{2,1,0:T(8,128)(2,1)} %copy-done.10), calls=%async_computation.1 | async-start | bytes 524288 | tf_op jit(solution)/shard_map/all_to_all | solution.py:67
  33.6 0.0 copy-done.15
  33.6 0.0 copy-done
  33.6 0.0 copy-done.2
  33.6 0.0 copy-done.4
  33.6 4.4 %within.1.a_ref = f32[512,1024]{1,0:T(8,128)S(1)} custom-call(bf16[512,1024]{1,0:T(8,128)(2,1)S(1)} %copy-done, bf16[512,1024]{1,0:T(8,128)(2,1)S(1)} %copy-done.2, bf16[512,1024]{1,0:T(8,128)(2,1)S(1)} %copy-done.4), custom_call_target="tpu_custom_call" | custom-call | tf_op jit(solution)/shard_map/within/pallas_call | solution.py:115
  38.1 0.0 copy-start.6
  38.1 1.3 %copy-done.6 = f32[512,1024]{1,0:T(8,128)} copy-done((f32[512,1024]{1,0:T(8,128)}, f32[512,1024]{1,0:T(8,128)S(1)}, u32[]{:S(2)}) %copy-start.6) | copy-done | bytes 2097176
  39.4 4.6 %all-to-all-done.1 = bf16[32,32,128]{2,1,0:T(8,128)(2,1)S(1)} async-done(((bf16[32,32,128]{2,1,0:T(8,128)(2,1)}), bf16[32,32,128]{2,1,0:T(8,128)(2,1)S(1)}, u32[]{:S(2)}, u32[]{:S(2)}) %all-to-all-start.1) | async-done | bytes 262176 | tf_op jit(solution)/shard_map/all_to_all | solution.py:67
  44.0 0.0 copy-start.7
  44.0 1.2 %copy-done.7 = bf16[512,1024]{1,0:T(8,128)(2,1)S(1)} copy-done((bf16[512,1024]{1,0:T(8,128)(2,1)S(1)}, bf16[512,1024]{1,0:T(8,128)(2,1)}, u32[]{:S(2)}) %copy-start.7) | copy-done | bytes 1048600
  45.2 3.3 %attend.1 = (f32[512,1024]{1,0:T(8,128)S(1)}, f32[8,8,128]{2,1,0:T(8,128)S(1)}) custom-call(f32[512,1024]{1,0:T(8,128)} %copy-done.6, bf16[512,1024]{1,0:T(8,128)(2,1)S(1)} %copy-done, bf16[1024,128]{1,0:T(8,128)(2,1)S(1)} %bitcast.4, bf16[512,1024]{1,0:T(8,128)(2,1)S(1)} %copy-done.7, bf16[1,1024]{1,0:T(2,128)(2,1)S(1)} %reshape.25.gain_ref), custom_call_target="tpu_custom_call" | custom-call | tf_op jit(solution)/shard_map/attend/pallas_call | solution.py:157
  48.5 0.0 copy-start.5
  48.6 9.7 %all_to_all.26.stat_ref = f32[8,8,128]{2,1,0:T(8,128)S(1)} all-to-all(f32[8,8,128]{2,1,0:T(8,128)S(1)} %get-tuple-element.16), channel_id=1, replica_groups=mesh['ctx'=32,'head'=8] {'head'}, dimensions={0} | all-to-all | bytes 65536 | tf_op jit(solution)/shard_map/all_to_all | solution.py:67
  58.3 2.1 %grad.1 = (bf16[512,1024]{1,0:T(8,128)(2,1)S(1)}, bf16[1024,128]{1,0:T(8,128)(2,1)S(1)}, f32[512,128]{1,0:T(8,128)S(1)}) custom-call(f32[512,1024]{1,0:T(8,128)S(1)} %get-tuple-element.15.att_ref, bf16[512,1024]{1,0:T(8,128)(2,1)S(1)} %copy-done.7, bf16[1,1024]{1,0:T(2,128)(2,1)S(1)} %reshape.25.gain_ref, f32[8,8,128]{2,1,0:T(8,128)S(1)} %all_to_all.26.stat_ref, ...), custom_call_target="tpu_custom_call" | custom-call | tf_op jit(solution)/shard_map/grad/pallas_call | solution.py:205
  60.4 0.0 copy-done.5
  60.4 0.0 copy-start.11
  60.4 1.0 copy-done.11
  61.4 0.0 copy-start.13
  61.4 0.7 copy-done.13
  62.1 16.5 %all_to_all.27.x_ref = bf16[32,32,128]{2,1,0:T(8,128)(2,1)S(1)} all-to-all(bf16[32,32,128]{2,1,0:T(8,128)(2,1)S(1)} %bitcast.7), channel_id=1, replica_groups=mesh['ctx'=32,'head'=8] {'ctx'}, dimensions={0} | all-to-all | bytes 524288 | tf_op jit(solution)/shard_map/all_to_all | solution.py:67
  78.6 0.0 copy-start.9
  78.6 0.7 copy-done.9
  79.3 5.9 %all-to-all-start.4 = ((bf16[32,32,128]{2,1,0:T(8,128)(2,1)}), bf16[32,32,128]{2,1,0:T(8,128)(2,1)}, u32[]{:S(2)}, u32[]{:S(2)}) async-start(bf16[32,32,128]{2,1,0:T(8,128)(2,1)} %copy-done.9), calls=%async_computation.4 | async-start | bytes 524288 | tf_op jit(solution)/shard_map/all_to_all | solution.py:67
  85.2 0.0 copy-start.12
  85.2 1.2 %copy-done.12 = bf16[512,1024]{1,0:T(8,128)(2,1)S(1)} copy-done((bf16[512,1024]{1,0:T(8,128)(2,1)S(1)}, bf16[512,1024]{1,0:T(8,128)(2,1)}, u32[]{:S(2)}) %copy-start.12) | copy-done | bytes 1048600
  86.5 0.0 copy-start.14
  86.5 0.9 copy-done.14
  87.4 10.8 %side.1 = (bf16[512,1024]{1,0:T(8,128)(2,1)}, bf16[512,1024]{1,0:T(8,128)(2,1)}, f32[512,1024]{1,0:T(8,128)}, f32[512,1024]{1,0:T(8,128)}) custom-call(bf16[512,1024]{1,0:T(8,128)(2,1)S(1)} %copy-done, bf16[512,1024]{1,0:T(8,128)(2,1)S(1)} %copy-done.2, bf16[512,1024]{1,0:T(8,128)(2,1)S(1)} %copy-done.4, bf16[512,1024]{1,0:T(8,128)(2,1)S(1)} %copy-done.12, ...), custom_call_target="tpu_custom_call" | custom-call | tf_op jit(solution)/shard_map/side/pallas_call | solution.py:246
  98.2 0.0 all-to-all-done.4
  98.2 0.0 copy-start.8
  98.2 1.6 %copy-done.8 = f32[512,1024]{1,0:T(8,128)S(1)} copy-done((f32[512,1024]{1,0:T(8,128)S(1)}, f32[512,1024]{1,0:T(8,128)}, u32[]{:S(2)}) %copy-start.8) | copy-done | bytes 2097176
  99.8 4.3 %last.1 = (bf16[512,1024]{1,0:T(8,128)(2,1)}, bf16[512,1024]{1,0:T(8,128)(2,1)}) custom-call(f32[512,1024]{1,0:T(8,128)S(1)} %copy-done.8, f32[512,1024]{1,0:T(8,128)} %get-tuple-element.22.gv_ref, bf16[512,1024]{1,0:T(8,128)(2,1)S(1)} %copy-done.2, bf16[512,1024]{1,0:T(8,128)(2,1)S(1)} %copy-done.4, bf16[1024,128]{1,0:T(8,128)(2,1)} %bitcast.3.s_ref), custom_call_target="tpu_custom_call" | custom-call | tf_op jit(solution)/shard_map/last/pallas_call | solution.py:282
  (3 shorter events, 0.1 us)
Async XLA Ops:
  0.6 33.0 %copy-start = (bf16[512,1024]{1,0:T(8,128)(2,1)S(1)}, bf16[512,1024]{1,0:T(8,128)(2,1)}, u32[]{:S(2)}) copy-start(bf16[512,1024]{1,0:T(8,128)(2,1)} %q_ref.7) | copy-start | bytes 3145732
  0.6 1.3 %copy-start.1 = (bf16[512,1024]{1,0:T(8,128)(2,1)S(1)}, bf16[512,1024]{1,0:T(8,128)(2,1)}, u32[]{:S(2)}) copy-start(bf16[512,1024]{1,0:T(8,128)(2,1)} %k_ref.5) | copy-start | bytes 3145732
  2.0 1.2 %copy-start.3 = (bf16[512,1024]{1,0:T(8,128)(2,1)S(1)}, bf16[512,1024]{1,0:T(8,128)(2,1)}, u32[]{:S(2)}) copy-start(bf16[512,1024]{1,0:T(8,128)(2,1)} %v_ref.5) | copy-start | bytes 3145732
  3.2 30.4 %copy-start.15 = (bf16[1024]{0:T(1024)(128)(2,1)S(1)}, bf16[1024]{0:T(1024)(128)(2,1)}, u32[]{:S(2)}) copy-start(bf16[1024]{0:T(1024)(128)(2,1)} %param.8) | copy-start | bytes 6148
  3.2 30.4 %copy-start.2 = (bf16[512,1024]{1,0:T(8,128)(2,1)S(1)}, bf16[512,1024]{1,0:T(8,128)(2,1)}, u32[]{:S(2)}) copy-start(bf16[512,1024]{1,0:T(8,128)(2,1)} %k_ref.5) | copy-start | bytes 3145732
  3.2 30.4 %copy-start.4 = (bf16[512,1024]{1,0:T(8,128)(2,1)S(1)}, bf16[512,1024]{1,0:T(8,128)(2,1)}, u32[]{:S(2)}) copy-start(bf16[512,1024]{1,0:T(8,128)(2,1)} %v_ref.5) | copy-start | bytes 3145732
  27.3 0.7 copy-start.10
  28.0 16.0 %all-to-all-start.1 = ((bf16[32,32,128]{2,1,0:T(8,128)(2,1)}), bf16[32,32,128]{2,1,0:T(8,128)(2,1)S(1)}, u32[]{:S(2)}, u32[]{:S(2)}) async-start(bf16[32,32,128]{2,1,0:T(8,128)(2,1)} %copy-done.10), calls=%async_computation.1 | async-start | bytes 524288 | tf_op jit(solution)/shard_map/all_to_all | solution.py:67
  38.1 1.3 %copy-start.6 = (f32[512,1024]{1,0:T(8,128)}, f32[512,1024]{1,0:T(8,128)S(1)}, u32[]{:S(2)}) copy-start(f32[512,1024]{1,0:T(8,128)S(1)} %within.1.a_ref) | copy-start | bytes 6291460
  44.0 1.2 %copy-start.7 = (bf16[512,1024]{1,0:T(8,128)(2,1)S(1)}, bf16[512,1024]{1,0:T(8,128)(2,1)}, u32[]{:S(2)}) copy-start(bf16[512,1024]{1,0:T(8,128)(2,1)} %cot_ref.3) | copy-start | bytes 3145732
  48.5 11.9 %copy-start.5 = (f32[512,1024]{1,0:T(8,128)}, f32[512,1024]{1,0:T(8,128)S(1)}, u32[]{:S(2)}) copy-start(f32[512,1024]{1,0:T(8,128)S(1)} %get-tuple-element.15.att_ref) | copy-start | bytes 6291460
  60.4 1.0 copy-start.11
  61.4 0.7 copy-start.13
  78.6 0.7 copy-start.9
  79.3 18.9 %all-to-all-start.4 = ((bf16[32,32,128]{2,1,0:T(8,128)(2,1)}), bf16[32,32,128]{2,1,0:T(8,128)(2,1)}, u32[]{:S(2)}, u32[]{:S(2)}) async-start(bf16[32,32,128]{2,1,0:T(8,128)(2,1)} %copy-done.9), calls=%async_computation.4 | async-start | bytes 524288 | tf_op jit(solution)/shard_map/all_to_all | solution.py:67
  85.2 1.2 %copy-start.12 = (bf16[512,1024]{1,0:T(8,128)(2,1)S(1)}, bf16[512,1024]{1,0:T(8,128)(2,1)}, u32[]{:S(2)}) copy-start(bf16[512,1024]{1,0:T(8,128)(2,1)} %copy-done.11) | copy-start | bytes 3145732
  86.5 0.9 copy-start.14
  98.2 1.6 %copy-start.8 = (f32[512,1024]{1,0:T(8,128)S(1)}, f32[512,1024]{1,0:T(8,128)}, u32[]{:S(2)}) copy-start(f32[512,1024]{1,0:T(8,128)} %get-tuple-element.21.gk_ref) | copy-start | bytes 6291460

commit v2 on v0

v2 whole, which is shorter than its diff:
```python
import functools

import jax
import jax.numpy as jnp
from jax import lax
from jax.experimental import pallas as pl
from jax.experimental.pallas import tpu as pltpu
from jax.sharding import PartitionSpec as P

DH = 128
F32 = jnp.float32
BF16 = jnp.bfloat16
VMEM_LIMIT = 16 * 1024 * 1024
VMEM_MOST = 60 * 1024 * 1024
VMEM = pl.BlockSpec(memory_space=pltpu.VMEM)


def far(x):
    return pltpu.with_memory_space_constraint(x, pltpu.HBM)


NT = (((1,), (1,)), ((), ()))
NN = (((1,), (0,)), ((), ()))
TN = (((0,), (0,)), ((), ()))


def dot(a, b, dims):
    return lax.dot_general(a, b, dims, preferred_element_type=F32)


def params(limit=VMEM_LIMIT):
    return pltpu.CompilerParams(vmem_limit_bytes=limit)


def heads_of(ref):
    return [slice(c, c + DH) for c in range(0, ref.shape[1], DH)]


HBM = pl.BlockSpec(memory_space=pltpu.HBM)


class Mover:
    def __init__(self, sems):
        self.sems = sems
        self.used = 0

    def start(self, src, dst):
        copy = pltpu.make_async_copy(src, dst, self.sems.at[self.used])
        self.used += 1
        copy.start()
        return copy


def chunks_of(ref, step):
    return [slice(r, r + step) for r in range(0, ref.shape[0], step)]


def groups_of(ref, step):
    return [slice(c, c + step) for c in range(0, ref.shape[1], step)]


def outer_kernel(a_hbm, b_hbm, out_hbm, a_ref, b_ref, acc_ref, out_ref, sems, *, step):
    mover = Mover(sems)
    chunks = chunks_of(a_ref, step)
    loads = [
        (mover.start(a_hbm.at[rows], a_ref.at[rows]), mover.start(b_hbm.at[rows], b_ref.at[rows])) for rows in chunks
    ]
    for i, rows in enumerate(chunks):
        for copy in loads[i]:
            copy.wait()
        for cols in heads_of(a_ref):
            term = dot(a_ref[rows, cols], b_ref[rows, cols], TN)
            if i > 0:
                term = acc_ref[cols, :] + term
            if i < len(chunks) - 1:
                acc_ref[cols, :] = term
            else:
                out_ref[cols, :] = term.astype(BF16)
    mover.start(out_ref, out_hbm).wait()


def outer(a, b, step):
    rows, width = a.shape
    return pl.pallas_call(
        functools.partial(outer_kernel, step=step),
        in_specs=[HBM] * 2,
        out_specs=HBM,
        out_shape=pltpu.HBM((width, DH), BF16),
        scratch_shapes=[
            pltpu.VMEM((rows, width), BF16),
            pltpu.VMEM((rows, width), BF16),
            pltpu.VMEM((width, DH), F32),
            pltpu.VMEM((width, DH), BF16),
            pltpu.SemaphoreType.DMA((2 * rows // step + 1,)),
        ],
        compiler_params=params(VMEM_MOST),
        name="outer",
    )(far(a), far(b))


def scan_kernel(x_ref, out_ref, *, backward):
    count = x_ref.shape[0]
    total = jnp.zeros(x_ref.shape[1:], F32)
    for lap in range(count):
        i = count - 1 - lap if backward else lap
        out_ref[i] = total.astype(BF16)
        total = total + x_ref[i].astype(F32)


def scan(x, backward):
    return pl.pallas_call(
        functools.partial(scan_kernel, backward=backward),
        out_shape=jax.ShapeDtypeStruct(x.shape, BF16),
        compiler_params=params(),
        name="suffix" if backward else "prefix",
    )(x)


def exchange(x, axis):
    return lax.all_to_all(x, axis, 0, 0)


def keep_lower(x):
    row = lax.broadcasted_iota(jnp.int32, x.shape, 0)
    col = lax.broadcasted_iota(jnp.int32, x.shape, 1)
    return jnp.where(row >= col, x, 0.0)


def keep_upper(x):
    row = lax.broadcasted_iota(jnp.int32, x.shape, 0)
    col = lax.broadcasted_iota(jnp.int32, x.shape, 1)
    return jnp.where(row <= col, x, 0.0)


def lower_product(a, b, c):
    half = a.shape[0] // 2
    top = keep_lower(dot(a[:half], b[:half], NT)).astype(BF16)
    low = dot(a[half:], b[:half], NT).astype(BF16)
    last = keep_lower(dot(a[half:], b[half:], NT)).astype(BF16)
    return dot(top, c[:half], NN), dot(low, c[:half], NN) + dot(last, c[half:], NN)


def upper_product(a, b, c):
    half = a.shape[0] // 2
    top = keep_upper(dot(a[:half], b[:half], NT)).astype(BF16)
    high = dot(a[:half], b[half:], NT).astype(BF16)
    last = keep_upper(dot(a[half:], b[half:], NT)).astype(BF16)
    return dot(top, c[:half], NN) + dot(high, c[half:], NN), dot(last, c[half:], NN)


def within_kernel(q_hbm, k_hbm, v_hbm, out_hbm, q_ref, k_ref, v_ref, out_ref, sems):
    mover = Mover(sems)
    half = q_ref.shape[0] // 2
    loads = [mover.start(src, dst) for src, dst in ((q_hbm, q_ref), (k_hbm, k_ref), (v_hbm, v_ref))]
    for copy in loads:
        copy.wait()
    for cols in heads_of(q_ref):
        one, two = lower_product(q_ref[:, cols], k_ref[:, cols], v_ref[:, cols])
        out_ref[:half, cols] = one
        out_ref[half:, cols] = two
    mover.start(out_ref, out_hbm).wait()


def within(q, k, v):
    return pl.pallas_call(
        within_kernel,
        in_specs=[HBM] * 3,
        out_specs=HBM,
        out_shape=pltpu.HBM(q.shape, F32),
        scratch_shapes=[pltpu.VMEM(q.shape, BF16)] * 3 + [pltpu.VMEM(q.shape, F32), pltpu.SemaphoreType.DMA((4,))],
        compiler_params=params(VMEM_MOST),
        name="within",
    )(far(q), far(k), far(v))


def attend_kernel(a_hbm, q_ref, s_ref, cot_ref, gain_ref, att_ref, stat_ref, a_ref, sems):
    mover = Mover(sems)
    rows = q_ref.shape[0]
    chunks = chunks_of(q_ref, DH)
    loads = [mover.start(a_hbm.at[span], a_ref.at[span]) for span in chunks]
    for cols in heads_of(q_ref):
        att_ref[:, cols] = dot(q_ref[:, cols], s_ref[cols, :], NN)
    for i, span in enumerate(chunks):
        loads[i].wait()
        sq = jnp.zeros((DH, DH), F32)
        cr = jnp.zeros((DH, DH), F32)
        for cols in heads_of(q_ref):
            att = a_ref[span, cols] + att_ref[span, cols]
            att_ref[span, cols] = att
            scaled = cot_ref[span, cols].astype(F32) * gain_ref[:, cols].astype(F32)
            sq += att * att
            cr += scaled * att
        for j, part in enumerate((sq, cr)):
            line = jnp.sum(part.T, axis=0, keepdims=True)
            for copy in range(stat_ref.shape[0]):
                stat_ref[copy, j * len(chunks) + i : j * len(chunks) + i + 1, :] = line


def attend(a, q, s, cot, gain, copies):
    rows, width = q.shape
    vmem = pl.BlockSpec(memory_space=pltpu.VMEM)
    return pl.pallas_call(
        attend_kernel,
        in_specs=[HBM] + [vmem] * 4,
        out_shape=[
            jax.ShapeDtypeStruct((rows, width), F32),
            jax.ShapeDtypeStruct((copies, 2 * rows // DH, DH), F32),
        ],
        scratch_shapes=[pltpu.VMEM((rows, width), F32), pltpu.SemaphoreType.DMA((rows // DH,))],
        compiler_params=params(),
        name="attend",
    )(far(a), q, s, cot, gain)


def grad_kernel(
    att_ref, cot_ref, gain_ref, stat_ref, q_ref, g_hbm, lg_hbm, n_hbm, g_ref, lg_ref, n_ref, sems, *, total
):
    mover = Mover(sems)
    rows = att_ref.shape[0]
    blocks = rows // DH
    stats = jnp.sum(stat_ref[...], axis=0) / total
    inv = lax.rsqrt(stats[:blocks] + 1e-06)
    pull = inv**3 * stats[blocks:]
    stores = []
    for i, span in enumerate(chunks_of(att_ref, DH)):
        inv_tile = jnp.broadcast_to(inv[i : i + 1], (DH, DH)).T
        pull_tile = jnp.broadcast_to(pull[i : i + 1], (DH, DH)).T
        for cols in heads_of(q_ref):
            gain = gain_ref[:, cols].astype(F32)
            att = att_ref[span, cols]
            scaled = cot_ref[span, cols].astype(F32) * gain
            g_ref[span, cols] = (inv_tile * scaled - att * pull_tile).astype(BF16)
            n_ref[span, cols] = (att * inv_tile * gain).astype(BF16)
        stores.append(mover.start(g_ref.at[span], g_hbm.at[span]))
        stores.append(mover.start(n_ref.at[span], n_hbm.at[span]))
    for cols in heads_of(q_ref):
        lg_ref[cols, :] = dot(q_ref[:, cols], g_ref[:, cols], TN).astype(BF16)
    stores.append(mover.start(lg_ref, lg_hbm))
    for copy in stores:
        copy.wait()


def grad(att, cot, gain, stats, q, total):
    rows, width = q.shape
    shapes = [(rows, width), (width, DH), (rows, width)]
    return pl.pallas_call(
        functools.partial(grad_kernel, total=total),
        out_specs=[HBM] * 3,
        out_shape=[pltpu.HBM(shape, BF16) for shape in shapes],
        scratch_shapes=[pltpu.VMEM(shape, BF16) for shape in shapes]
        + [pltpu.SemaphoreType.DMA((2 * rows // DH + 1,))],
        compiler_params=params(),
        name="grad",
    )(att, cot, gain, stats, q)


def side_kernel(q_hbm, k_hbm, v_hbm, g_hbm, s_hbm, *refs, step):
    gq_hbm, gk_hbm, gv_hbm, q_ref, k_ref, v_ref, g_ref, s_ref, gq_ref, gk_ref, gv_ref, sems = refs
    mover = Mover(sems)
    half = q_ref.shape[0] // 2
    groups = groups_of(q_ref, step)
    here = step // DH
    s_in = mover.start(s_hbm, s_ref)
    pairs = ((g_hbm, g_ref), (v_hbm, v_ref), (k_hbm, k_ref), (q_hbm, q_ref))
    loads = [[mover.start(src.at[:, group], dst.at[:, group]) for src, dst in pairs] for group in groups]
    stores = []
    s_in.wait()
    for i, group in enumerate(groups):
        for copy in loads[i]:
            copy.wait()
        spans = heads_of(q_ref)[i * here : (i + 1) * here]
        for cols in spans:
            one, two = upper_product(v_ref[:, cols], g_ref[:, cols], q_ref[:, cols])
            gk_ref[:half, cols] = one
            gk_ref[half:, cols] = two
        stores.append(mover.start(gk_ref.at[:, group], gk_hbm.at[:, group]))
        for cols in spans:
            one, two = upper_product(k_ref[:, cols], q_ref[:, cols], g_ref[:, cols])
            gv_ref[:half, cols] = one
            gv_ref[half:, cols] = two
        stores.append(mover.start(gv_ref.at[:, group], gv_hbm.at[:, group]))
        for cols in spans:
            g = g_ref[:, cols]
            one, two = lower_product(g, v_ref[:, cols], k_ref[:, cols])
            rest = dot(g, s_ref[cols, :], NT)
            gq_ref[:half, cols] = (one + rest[:half]).astype(BF16)
            gq_ref[half:, cols] = (two + rest[half:]).astype(BF16)
        stores.append(mover.start(gq_ref.at[:, group], gq_hbm.at[:, group]))
    for copy in stores:
        copy.wait()


def side(q, k, v, g, s, step):
    outs = [pltpu.HBM(q.shape, kind) for kind in (BF16, F32, F32)]
    ins = (q, k, v, g, s)
    return pl.pallas_call(
        functools.partial(side_kernel, step=step),
        in_specs=[HBM] * len(ins),
        out_specs=[HBM] * len(outs),
        out_shape=outs,
        scratch_shapes=[pltpu.VMEM(x.shape, x.dtype) for x in (*ins, *outs)]
        + [pltpu.SemaphoreType.DMA((1 + 7 * q.shape[1] // step,))],
        compiler_params=params(VMEM_MOST),
        name="side",
    )(*[far(x) for x in ins])


def last_kernel(gk_hbm, gv_hbm, k_ref, v_ref, s_ref, outk_hbm, outv_hbm, gk_ref, gv_ref, outk_ref, outv_ref, sems, *, step):
    mover = Mover(sems)
    chunks = chunks_of(k_ref, step)
    loads = [
        (mover.start(gk_hbm.at[rows], gk_ref.at[rows]), mover.start(gv_hbm.at[rows], gv_ref.at[rows]))
        for rows in chunks
    ]
    stores = []
    for i, rows in enumerate(chunks):
        loads[i][0].wait()
        for cols in heads_of(k_ref):
            far = dot(v_ref[rows, cols], s_ref[cols, :], NT)
            outk_ref[rows, cols] = (gk_ref[rows, cols] + far).astype(BF16)
        stores.append(mover.start(outk_ref.at[rows], outk_hbm.at[rows]))
        loads[i][1].wait()
        for cols in heads_of(k_ref):
            far = dot(k_ref[rows, cols], s_ref[cols, :], NN)
            outv_ref[rows, cols] = (gv_ref[rows, cols] + far).astype(BF16)
        stores.append(mover.start(outv_ref.at[rows], outv_hbm.at[rows]))
    for copy in stores:
        copy.wait()


def last(gk, gv, k, v, s, step):
    rows, width = k.shape
    vmem = pl.BlockSpec(memory_space=pltpu.VMEM)
    return pl.pallas_call(
        functools.partial(last_kernel, step=step),
        in_specs=[HBM] * 2 + [vmem] * 3,
        out_specs=[HBM] * 2,
        out_shape=[jax.ShapeDtypeStruct((rows, width), BF16)] * 2,
        scratch_shapes=[pltpu.VMEM((rows, width), F32)] * 2
        + [pltpu.VMEM((rows, width), BF16)] * 2
        + [pltpu.SemaphoreType.DMA((4 * rows // step,))],
        compiler_params=params(),
        name="last",
    )(far(gk), far(gv), k, v, s)


def body(queries, keys, values, gain, cotangent):
    rows, width = queries.shape
    count, heads = lax.axis_size("ctx"), lax.axis_size("head")
    gain = gain.reshape(1, width)
    parts = (count, width // count, DH)

    local = exchange(outer(keys, values, 256).reshape(parts), "ctx")
    a = within(queries, keys, values)
    local, a, gain = lax.optimization_barrier((local, a, gain))
    state = exchange(scan(local, False), "ctx").reshape(width, DH)

    att, stats = attend(a, queries, state, cotangent, gain, heads)
    stats = exchange(stats, "head")
    g, local, normed = grad(att, cotangent, gain, stats, queries, width * heads)

    local = exchange(local.reshape(parts), "ctx")
    sides = side(queries, keys, values, g, state, 256)
    local, grad_q, gk, gv = lax.optimization_barrier((local, *sides))
    later = exchange(scan(local, True), "ctx").reshape(width, DH)
    grad_k, grad_v = last(gk, gv, keys, values, later, 256)
    return normed, grad_q, grad_k, grad_v


def solution(mesh):
    return jax.shard_map(
        body,
        mesh=mesh,
        in_specs=(
            P("ctx", "head"),
            P("ctx", "head"),
            P("ctx", "head"),
            P("head"),
            P("ctx", "head"),
        ),
        out_specs=(P("ctx", "head"), P("ctx", "head"), P("ctx", "head"), P("ctx", "head")),
        check_vma=False,
    )
```

time: 323 us -> 95.8 us (0.30)
  waiting for transfers between devices: 204 us -> 7.67 us
  other arithmetic: 38.8 us -> 0 us
  blocking collectives: 14.2 us -> 43.9 us
  matrix products: 27.6 us -> 0 us
  Pallas kernels: 0 us -> 25 us
  local copies, waits for them, and re-layouts: 19.8 us -> 0.04 us
  starting transfers between devices: 0.08 us -> 17.4 us
  between operations: 14.3 us -> 0.92 us
    all_gather x2 -> x0, waiting for transfers between devices: 204 us -> none  [prefix_2(): gathered = lax.all_gather(x.astype(jnp.bfloat16), axis)]
    all_to_all x0 -> x3, blocking collectives: none -> 43.9 us  [exchange(): return lax.all_to_all(x, axis, 0, 0)]
    add x31 -> x0, other arithmetic: 33.2 us -> none  [add_states(): return earlier + latter]
    dot_general x12 -> x0, matrix products: 27.6 us -> none  [the longest x1 4.23 us: body(): jnp.einsum('hts,thd->shd', attn, g_heads, preferred_element_type=jnp.floa...]
    pallas_call x0 -> x8, Pallas kernels: none -> 25 us  [the longest x1 9.36 us: side(): pl.pallas_call(functools.partial(side_kernel, step=step), in_specs=[HBM]...]
    all_to_all x0 -> x2, starting transfers between devices: none -> 17.4 us  [exchange(): return lax.all_to_all(x, axis, 0, 0)]
    psum x1 -> x0, blocking collectives: 14.2 us -> none  [body(): lax.psum((jnp.sum(attended * attended, axis=1), jnp.sum(scaled * attended...]
    unnamed x28 -> x12, local copies, waits for them, and re-layouts: 12.8 us -> 0.03 us
  transfers between devices with their start and end apart: 2 -> 2, of which waited for: 2 -> 2; matrix products, arithmetic and copies ran while one was open for 6% -> 0% of each run, Pallas kernels for 0% -> 16%
where the time goes in v2:
time: 95.8 us; the launch traced here: 94.9 us
  blocking collectives  43.9 us (46%)
  Pallas kernels  25 us (26%)
  starting transfers between devices  17.4 us (18%)
  waiting for transfers between devices  7.67 us (8%)
    all_to_all x3, blocking collectives, exchange(): return lax.all_to_all(x, axis, 0, 0)  43.9 us
    all_to_all x2, starting transfers between devices, exchange(): return lax.all_to_all(x, axis, 0, 0)  17.4 us
    pallas_call x1, Pallas kernels, side(): pl.pallas_call(functools.partial(side_kernel, step=step), in_specs=[HBM]...  9.36 us
    all_to_all x2, waiting for transfers between devices, exchange(): return lax.all_to_all(x, axis, 0, 0)  7.67 us
    pallas_call x1, Pallas kernels, within(): pl.pallas_call(within_kernel, in_specs=[HBM] * 3, out_specs=HBM, out_shap...  5.61 us
    pallas_call x1, Pallas kernels, last(): pl.pallas_call(functools.partial(last_kernel, step=step), in_specs=[HBM]...  3.32 us
    pallas_call x1, Pallas kernels, outer(): pl.pallas_call(functools.partial(outer_kernel, step=step), in_specs=[HBM]...  2.66 us
    pallas_call x1, Pallas kernels, attend(): pl.pallas_call(attend_kernel, in_specs=[HBM] + [vmem] * 4, out_shape=[jax...  2.01 us
  transfers between devices with their start and end apart: 2, of which 2 were waited for; matrix products, arithmetic and copies ran while one was open for 0% of the time, Pallas kernels for 16%

profile of v2, /device:TPU:2, one launch (start us, length us, event | category | flops | bytes accessed | tf_op | source)
XLA Modules:
  0.0 94.9 jit_solution(18032402066899968778)
XLA Ops:
  0.6 0.0 copy-start.5
  0.6 2.7 %outer.1 = bf16[1024,128]{1,0:T(8,128)(2,1)} custom-call(bf16[512,1024]{1,0:T(8,128)(2,1)} %k_ref.1, bf16[512,1024]{1,0:T(8,128)(2,1)} %v_ref.1), custom_call_target="tpu_custom_call" | custom-call | tf_op jit(solution)/shard_map/outer/pallas_call | solution.py:84
  3.3 11.6 %all-to-all-start = ((bf16[32,32,128]{2,1,0:T(8,128)(2,1)}), bf16[32,32,128]{2,1,0:T(8,128)(2,1)S(1)}, u32[]{:S(2)}, u32[]{:S(2)}) async-start(bf16[32,32,128]{2,1,0:T(8,128)(2,1)} %bitcast.7), calls=%async_computation | async-start | bytes 524288 | tf_op jit(solution)/shard_map/all_to_all | solution.py:120
  14.9 0.0 copy-done.5
  15.0 0.0 copy-start
  15.0 0.0 copy-start.3
  15.0 5.6 %within.1.a_hbm = f32[512,1024]{1,0:T(8,128)} custom-call(bf16[512,1024]{1,0:T(8,128)(2,1)} %q_hbm.3, bf16[512,1024]{1,0:T(8,128)(2,1)} %k_ref.1, bf16[512,1024]{1,0:T(8,128)(2,1)} %v_ref.1), custom_call_target="tpu_custom_call" | custom-call | tf_op jit(solution)/shard_map/within/pallas_call | solution.py:165
  20.6 5.5 %all-to-all-done.x_ref = bf16[32,32,128]{2,1,0:T(8,128)(2,1)S(1)} async-done(((bf16[32,32,128]{2,1,0:T(8,128)(2,1)}), bf16[32,32,128]{2,1,0:T(8,128)(2,1)S(1)}, u32[]{:S(2)}, u32[]{:S(2)}) %all-to-all-start) | async-done | bytes 262176 | tf_op jit(solution)/shard_map/all_to_all | solution.py:120
  26.2 15.8 %all_to_all.25 = bf16[32,32,128]{2,1,0:T(8,128)(2,1)S(1)} all-to-all(bf16[32,32,128]{2,1,0:T(8,128)(2,1)S(1)} %prefix.1), channel_id=1, replica_groups=mesh['ctx'=32,'head'=8] {'ctx'}, dimensions={0} | all-to-all | bytes 524288 | tf_op jit(solution)/shard_map/all_to_all | solution.py:120
  42.0 0.0 copy-start.4
  42.0 0.0 copy-done
  42.0 0.0 copy-done.3
  42.0 2.0 %attend.1 = (f32[512,1024]{1,0:T(8,128)S(1)}, f32[8,8,128]{2,1,0:T(8,128)S(1)}) custom-call(f32[512,1024]{1,0:T(8,128)} %within.1.a_hbm, bf16[512,1024]{1,0:T(8,128)(2,1)S(1)} %copy-done, bf16[1024,128]{1,0:T(8,128)(2,1)S(1)} %bitcast.4, bf16[512,1024]{1,0:T(8,128)(2,1)S(1)} %copy-done.3, bf16[1,1024]{1,0:T(2,128)(2,1)S(1)} %reshape.24.gain_ref), custom_call_target="tpu_custom_call" | custom-call | tf_op jit(solution)/shard_map/attend/pallas_call | solution.py:202
  44.0 0.0 copy-done.4
  44.0 9.7 %all_to_all.26.stat_ref = f32[8,8,128]{2,1,0:T(8,128)S(1)} all-to-all(f32[8,8,128]{2,1,0:T(8,128)S(1)} %get-tuple-element.25), channel_id=1, replica_groups=mesh['ctx'=32,'head'=8] {'head'}, dimensions={0} | all-to-all | bytes 65536 | tf_op jit(solution)/shard_map/all_to_all | solution.py:120
  53.7 1.9 %grad.1 = (bf16[512,1024]{1,0:T(8,128)(2,1)}, bf16[1024,128]{1,0:T(8,128)(2,1)}, bf16[512,1024]{1,0:T(8,128)(2,1)}) custom-call(f32[512,1024]{1,0:T(8,128)S(1)} %get-tuple-element.24.att_ref, bf16[512,1024]{1,0:T(8,128)(2,1)S(1)} %copy-done.3, bf16[1,1024]{1,0:T(2,128)(2,1)S(1)} %reshape.24.gain_ref, f32[8,8,128]{2,1,0:T(8,128)S(1)} %all_to_all.26.stat_ref, ...), custom_call_target="tpu_custom_call" | custom-call | tf_op jit(solution)/shard_map/grad/pallas_call | solution.py:246
  55.7 5.8 %all-to-all-start.3 = ((bf16[32,32,128]{2,1,0:T(8,128)(2,1)}), bf16[32,32,128]{2,1,0:T(8,128)(2,1)S(1)}, u32[]{:S(2)}, u32[]{:S(2)}) async-start(bf16[32,32,128]{2,1,0:T(8,128)(2,1)} %bitcast.8), calls=%async_computation.3 | async-start | bytes 524288 | tf_op jit(solution)/shard_map/all_to_all | solution.py:120
  61.4 0.0 copy-start.1
  61.5 0.0 copy-start.2
  61.5 9.4 %side.1 = (bf16[512,1024]{1,0:T(8,128)(2,1)}, f32[512,1024]{1,0:T(8,128)}, f32[512,1024]{1,0:T(8,128)}) custom-call(bf16[512,1024]{1,0:T(8,128)(2,1)} %q_hbm.3, bf16[512,1024]{1,0:T(8,128)(2,1)} %k_ref.1, bf16[512,1024]{1,0:T(8,128)(2,1)} %v_ref.1, bf16[512,1024]{1,0:T(8,128)(2,1)} %get-tuple-element.28.g_hbm, bf16[1024,128]{1,0:T(8,128)(2,1)} %bitcast.5), custom_call_target="tpu_custom_call" | custom-call | tf_op jit(solution)/shard_map/side/pallas_call | solution.py:296
  70.8 2.1 %all-to-all-done.3.x_ref = bf16[32,32,128]{2,1,0:T(8,128)(2,1)S(1)} async-done(((bf16[32,32,128]{2,1,0:T(8,128)(2,1)}), bf16[32,32,128]{2,1,0:T(8,128)(2,1)S(1)}, u32[]{:S(2)}, u32[]{:S(2)}) %all-to-all-start.3) | async-done | bytes 262176 | tf_op jit(solution)/shard_map/all_to_all | solution.py:120
  73.0 18.4 %all_to_all.27 = bf16[32,32,128]{2,1,0:T(8,128)(2,1)S(1)} all-to-all(bf16[32,32,128]{2,1,0:T(8,128)(2,1)S(1)} %suffix.1), channel_id=1, replica_groups=mesh['ctx'=32,'head'=8] {'ctx'}, dimensions={0} | all-to-all | bytes 524288 | tf_op jit(solution)/shard_map/all_to_all | solution.py:120
  91.5 0.0 copy-done.1
  91.5 0.0 copy-done.2
  91.5 3.3 %last.1 = (bf16[512,1024]{1,0:T(8,128)(2,1)}, bf16[512,1024]{1,0:T(8,128)(2,1)}) custom-call(f32[512,1024]{1,0:T(8,128)} %get-tuple-element.33.gk_hbm, f32[512,1024]{1,0:T(8,128)} %get-tuple-element.34.gv_hbm, bf16[512,1024]{1,0:T(8,128)(2,1)S(1)} %copy-done.1, bf16[512,1024]{1,0:T(8,128)(2,1)S(1)} %copy-done.2, bf16[1024,128]{1,0:T(8,128)(2,1)S(1)} %bitcast.6), custom_call_target="tpu_custom_call" | custom-call | tf_op jit(solution)/shard_map/last/pallas_call | solution.py:334
  (3 shorter events, 0.1 us)
Async XLA Ops:
  0.6 14.3 %copy-start.5 = (bf16[1024]{0:T(1024)(128)(2,1)S(1)}, bf16[1024]{0:T(1024)(128)(2,1)}, u32[]{:S(2)}) copy-start(bf16[1024]{0:T(1024)(128)(2,1)} %param.8) | copy-start | bytes 6148
  3.3 22.8 %all-to-all-start = ((bf16[32,32,128]{2,1,0:T(8,128)(2,1)}), bf16[32,32,128]{2,1,0:T(8,128)(2,1)S(1)}, u32[]{:S(2)}, u32[]{:S(2)}) async-start(bf16[32,32,128]{2,1,0:T(8,128)(2,1)} %bitcast.7), calls=%async_computation | async-start | bytes 524288 | tf_op jit(solution)/shard_map/all_to_all | solution.py:120
  15.0 27.0 %copy-start = (bf16[512,1024]{1,0:T(8,128)(2,1)S(1)}, bf16[512,1024]{1,0:T(8,128)(2,1)}, u32[]{:S(2)}) copy-start(bf16[512,1024]{1,0:T(8,128)(2,1)} %q_hbm.3) | copy-start | bytes 3145732
  15.0 27.0 %copy-start.3 = (bf16[512,1024]{1,0:T(8,128)(2,1)S(1)}, bf16[512,1024]{1,0:T(8,128)(2,1)}, u32[]{:S(2)}) copy-start(bf16[512,1024]{1,0:T(8,128)(2,1)} %cot_ref.3) | copy-start | bytes 3145732
  42.0 2.0 %copy-start.4 = (bf16[32,32,128]{2,1,0:T(8,128)(2,1)}, bf16[32,32,128]{2,1,0:T(8,128)(2,1)S(1)}, u32[]{:S(2)}) copy-start(bf16[32,32,128]{2,1,0:T(8,128)(2,1)S(1)} %all_to_all.25) | copy-start | bytes 786436
  55.7 17.3 %all-to-all-start.3 = ((bf16[32,32,128]{2,1,0:T(8,128)(2,1)}), bf16[32,32,128]{2,1,0:T(8,128)(2,1)S(1)}, u32[]{:S(2)}, u32[]{:S(2)}) async-start(bf16[32,32,128]{2,1,0:T(8,128)(2,1)} %bitcast.8), calls=%async_computation.3 | async-start | bytes 524288 | tf_op jit(solution)/shard_map/all_to_all | solution.py:120
  61.4 30.0 %copy-start.1 = (bf16[512,1024]{1,0:T(8,128)(2,1)S(1)}, bf16[512,1024]{1,0:T(8,128)(2,1)}, u32[]{:S(2)}) copy-start(bf16[512,1024]{1,0:T(8,128)(2,1)} %k_ref.1) | copy-start | bytes 3145732
  61.5 30.0 %copy-start.2 = (bf16[512,1024]{1,0:T(8,128)(2,1)S(1)}, bf16[512,1024]{1,0:T(8,128)(2,1)}, u32[]{:S(2)}) copy-start(bf16[512,1024]{1,0:T(8,128)(2,1)} %v_ref.1) | copy-start | bytes 3145732

commit v3 on v2

--- a/solution.py
+++ b/solution.py
@@ -10,6 +10,8 @@
 DH = 128
 F32 = jnp.float32
 BF16 = jnp.bfloat16
+PART = F32
+SCAN_COST = 10_000_000_000
 VMEM_LIMIT = 16 * 1024 * 1024
 VMEM_MOST = 60 * 1024 * 1024
 VMEM = pl.BlockSpec(memory_space=pltpu.VMEM)
@@ -111,6 +113,7 @@
     return pl.pallas_call(
         functools.partial(scan_kernel, backward=backward),
         out_shape=jax.ShapeDtypeStruct(x.shape, BF16),
+        cost_estimate=pl.CostEstimate(flops=SCAN_COST, bytes_accessed=SCAN_COST // 300, transcendentals=0),
         compiler_params=params(),
         name="suffix" if backward else "prefix",
     )(x)
@@ -132,84 +135,109 @@
     return jnp.where(row <= col, x, 0.0)
 
 
-def lower_product(a, b, c):
+def lower_parts(a, b):
     half = a.shape[0] // 2
-    top = keep_lower(dot(a[:half], b[:half], NT)).astype(BF16)
-    low = dot(a[half:], b[:half], NT).astype(BF16)
-    last = keep_lower(dot(a[half:], b[half:], NT)).astype(BF16)
+    return (
+        keep_lower(dot(a[:half], b[:half], NT)).astype(BF16),
+        dot(a[half:], b[:half], NT).astype(BF16),
+        keep_lower(dot(a[half:], b[half:], NT)).astype(BF16),
+    )
+
+
+def upper_parts(a, b):
+    half = a.shape[0] // 2
+    return (
+        keep_upper(dot(a[:half], b[:half], NT)).astype(BF16),
+        dot(a[:half], b[half:], NT).astype(BF16),
+        keep_upper(dot(a[half:], b[half:], NT)).astype(BF16),
+    )
+
+
+def lower_apply(parts, c):
+    top, low, last = parts
+    half = top.shape[0]
     return dot(top, c[:half], NN), dot(low, c[:half], NN) + dot(last, c[half:], NN)
 
 
-def upper_product(a, b, c):
-    half = a.shape[0] // 2
-    top = keep_upper(dot(a[:half], b[:half], NT)).astype(BF16)
-    high = dot(a[:half], b[half:], NT).astype(BF16)
-    last = keep_upper(dot(a[half:], b[half:], NT)).astype(BF16)
+def upper_apply(parts, c):
+    top, high, last = parts
+    half = top.shape[0]
     return dot(top, c[:half], NN) + dot(high, c[half:], NN), dot(last, c[half:], NN)
 
 
-def within_kernel(q_hbm, k_hbm, v_hbm, out_hbm, q_ref, k_ref, v_ref, out_ref, sems):
-    mover = Mover(sems)
-    half = q_ref.shape[0] // 2
-    loads = [mover.start(src, dst) for src, dst in ((q_hbm, q_ref), (k_hbm, k_ref), (v_hbm, v_ref))]
-    for copy in loads:
+def upper_turned(parts, c):
+    top, high, last = parts
+    half = top.shape[0]
+    return dot(top, c[:half], TN), dot(high, c[:half], TN) + dot(last, c[half:], TN)
+
+
+def put(ref, cols, pair):
+    half = ref.shape[0] // 2
+    ref[:half, cols] = pair[0].astype(ref.dtype)
+    ref[half:, cols] = pair[1].astype(ref.dtype)
+
+
+def within_kernel(q_hbm, k_hbm, v_hbm, out_hbm, q_ref, k_ref, v_ref, out_ref, sems, *, step):
+    mover = Mover(sems)
+    groups = groups_of(q_ref, step)
+    pairs = ((q_hbm, q_ref), (k_hbm, k_ref), (v_hbm, v_ref))
+    loads = [[mover.start(src.at[:, group], dst.at[:, group]) for src, dst in pairs] for group in groups]
+    stores = []
+    for i, group in enumerate(groups):
+        for copy in loads[i]:
+            copy.wait()
+        spans = heads_of(q_ref)[i * step // DH : (i + 1) * step // DH]
+        parts = [lower_parts(q_ref[:, cols], k_ref[:, cols]) for cols in spans]
+        for cols, part in zip(spans, parts):
+            put(out_ref, cols, lower_apply(part, v_ref[:, cols]))
+        stores.append(mover.start(out_ref.at[:, group], out_hbm.at[:, group]))
+    for copy in stores:
         copy.wait()
-    for cols in heads_of(q_ref):
-        one, two = lower_product(q_ref[:, cols], k_ref[:, cols], v_ref[:, cols])
-        out_ref[:half, cols] = one
-        out_ref[half:, cols] = two
-    mover.start(out_ref, out_hbm).wait()
-
-
-def within(q, k, v):
-    return pl.pallas_call(
-        within_kernel,
+
+
+def within(q, k, v, step):
+    return pl.pallas_call(
+        functools.partial(within_kernel, step=step),
         in_specs=[HBM] * 3,
         out_specs=HBM,
         out_shape=pltpu.HBM(q.shape, F32),
-        scratch_shapes=[pltpu.VMEM(q.shape, BF16)] * 3 + [pltpu.VMEM(q.shape, F32), pltpu.SemaphoreType.DMA((4,))],
+        scratch_shapes=[pltpu.VMEM(q.shape, BF16)] * 3 + [pltpu.VMEM(q.shape, F32), pltpu.SemaphoreType.DMA((4 * q.shape[1] // step,))],
         compiler_params=params(VMEM_MOST),
         name="within",
     )(far(q), far(k), far(v))
 
 
-def attend_kernel(a_hbm, q_ref, s_ref, cot_ref, gain_ref, att_ref, stat_ref, a_ref, sems):
-    mover = Mover(sems)
-    rows = q_ref.shape[0]
+def attend_kernel(a_ref, q_ref, s_ref, cot_ref, gain_ref, att_ref, stat_ref, sum_ref):
     chunks = chunks_of(q_ref, DH)
-    loads = [mover.start(a_hbm.at[span], a_ref.at[span]) for span in chunks]
-    for cols in heads_of(q_ref):
-        att_ref[:, cols] = dot(q_ref[:, cols], s_ref[cols, :], NN)
     for i, span in enumerate(chunks):
-        loads[i].wait()
         sq = jnp.zeros((DH, DH), F32)
         cr = jnp.zeros((DH, DH), F32)
         for cols in heads_of(q_ref):
-            att = a_ref[span, cols] + att_ref[span, cols]
+            att = a_ref[span, cols] + dot(q_ref[span, cols], s_ref[cols, :], NN)
             att_ref[span, cols] = att
             scaled = cot_ref[span, cols].astype(F32) * gain_ref[:, cols].astype(F32)
             sq += att * att
             cr += scaled * att
-        for j, part in enumerate((sq, cr)):
-            line = jnp.sum(part.T, axis=0, keepdims=True)
-            for copy in range(stat_ref.shape[0]):
-                stat_ref[copy, j * len(chunks) + i : j * len(chunks) + i + 1, :] = line
+        sum_ref[i] = sq
+        sum_ref[len(chunks) + i] = cr
+    lines = [jnp.sum(sum_ref[i].T, axis=0, keepdims=True) for i in range(sum_ref.shape[0])]
+    lines = jnp.concatenate(lines, axis=0)
+    for copy in range(stat_ref.shape[0]):
+        stat_ref[copy] = lines
 
 
 def attend(a, q, s, cot, gain, copies):
     rows, width = q.shape
-    vmem = pl.BlockSpec(memory_space=pltpu.VMEM)
     return pl.pallas_call(
         attend_kernel,
-        in_specs=[HBM] + [vmem] * 4,
         out_shape=[
             jax.ShapeDtypeStruct((rows, width), F32),
             jax.ShapeDtypeStruct((copies, 2 * rows // DH, DH), F32),
         ],
-        scratch_shapes=[pltpu.VMEM((rows, width), F32), pltpu.SemaphoreType.DMA((rows // DH,))],
+        scratch_shapes=[pltpu.VMEM((2 * rows // DH, DH, DH), F32)],
         compiler_params=params(),
         name="attend",
-    )(far(a), q, s, cot, gain)
+    )(a, q, s, cot, gain)
 
 
 def grad_kernel(
@@ -270,28 +298,22 @@
             copy.wait()
         spans = heads_of(q_ref)[i * here : (i + 1) * here]
         for cols in spans:
-            one, two = upper_product(v_ref[:, cols], g_ref[:, cols], q_ref[:, cols])
-            gk_ref[:half, cols] = one
-            gk_ref[half:, cols] = two
-        stores.append(mover.start(gk_ref.at[:, group], gk_hbm.at[:, group]))
-        for cols in spans:
-            one, two = upper_product(k_ref[:, cols], q_ref[:, cols], g_ref[:, cols])
-            gv_ref[:half, cols] = one
-            gv_ref[half:, cols] = two
-        stores.append(mover.start(gv_ref.at[:, group], gv_hbm.at[:, group]))
-        for cols in spans:
-            g = g_ref[:, cols]
-            one, two = lower_product(g, v_ref[:, cols], k_ref[:, cols])
+            q, k, v, g = q_ref[:, cols], k_ref[:, cols], v_ref[:, cols], g_ref[:, cols]
+            pull = upper_parts(v, g)
+            attn = upper_parts(k, q)
             rest = dot(g, s_ref[cols, :], NT)
-            gq_ref[:half, cols] = (one + rest[:half]).astype(BF16)
-            gq_ref[half:, cols] = (two + rest[half:]).astype(BF16)
-        stores.append(mover.start(gq_ref.at[:, group], gq_hbm.at[:, group]))
+            put(gk_ref, cols, upper_apply(pull, q))
+            one, two = upper_turned(pull, k)
+            put(gq_ref, cols, (one + rest[:half], two + rest[half:]))
+            put(gv_ref, cols, upper_apply(attn, g))
+        for src, dst in ((gk_ref, gk_hbm), (gv_ref, gv_hbm), (gq_ref, gq_hbm)):
+            stores.append(mover.start(src.at[:, group], dst.at[:, group]))
     for copy in stores:
         copy.wait()
 
 
 def side(q, k, v, g, s, step):
-    outs = [pltpu.HBM(q.shape, kind) for kind in (BF16, F32, F32)]
+    outs = [pltpu.HBM(q.shape, kind) for kind in (BF16, PART, PART)]
     ins = (q, k, v, g, s)
     return pl.pallas_call(
         functools.partial(side_kernel, step=step),
@@ -305,43 +327,30 @@
     )(*[far(x) for x in ins])
 
 
-def last_kernel(gk_hbm, gv_hbm, k_ref, v_ref, s_ref, outk_hbm, outv_hbm, gk_ref, gv_ref, outk_ref, outv_ref, sems, *, step):
-    mover = Mover(sems)
-    chunks = chunks_of(k_ref, step)
-    loads = [
-        (mover.start(gk_hbm.at[rows], gk_ref.at[rows]), mover.start(gv_hbm.at[rows], gv_ref.at[rows]))
-        for rows in chunks
-    ]
+def last_kernel(gk_ref, gv_ref, k_ref, v_ref, s_ref, outk_hbm, outv_hbm, outk_ref, outv_ref, sems, *, step):
+    mover = Mover(sems)
     stores = []
-    for i, rows in enumerate(chunks):
-        loads[i][0].wait()
-        for cols in heads_of(k_ref):
-            far = dot(v_ref[rows, cols], s_ref[cols, :], NT)
-            outk_ref[rows, cols] = (gk_ref[rows, cols] + far).astype(BF16)
-        stores.append(mover.start(outk_ref.at[rows], outk_hbm.at[rows]))
-        loads[i][1].wait()
-        for cols in heads_of(k_ref):
-            far = dot(k_ref[rows, cols], s_ref[cols, :], NN)
-            outv_ref[rows, cols] = (gv_ref[rows, cols] + far).astype(BF16)
-        stores.append(mover.start(outv_ref.at[rows], outv_hbm.at[rows]))
+    for group in groups_of(k_ref, step):
+        for cols in heads_of(k_ref)[group.start // DH : group.stop // DH]:
+            s = s_ref[cols, :]
+            outk_ref[:, cols] = (gk_ref[:, cols] + dot(v_ref[:, cols], s, NT)).astype(BF16)
+            outv_ref[:, cols] = (gv_ref[:, cols] + dot(k_ref[:, cols], s, NN)).astype(BF16)
+        stores.append(mover.start(outk_ref.at[:, group], outk_hbm.at[:, group]))
+        stores.append(mover.start(outv_ref.at[:, group], outv_hbm.at[:, group]))
     for copy in stores:
         copy.wait()
 
 
 def last(gk, gv, k, v, s, step):
     rows, width = k.shape
-    vmem = pl.BlockSpec(memory_space=pltpu.VMEM)
     return pl.pallas_call(
         functools.partial(last_kernel, step=step),
-        in_specs=[HBM] * 2 + [vmem] * 3,
         out_specs=[HBM] * 2,
-        out_shape=[jax.ShapeDtypeStruct((rows, width), BF16)] * 2,
-        scratch_shapes=[pltpu.VMEM((rows, width), F32)] * 2
-        + [pltpu.VMEM((rows, width), BF16)] * 2
-        + [pltpu.SemaphoreType.DMA((4 * rows // step,))],
+        out_shape=[pltpu.HBM((rows, width), BF16)] * 2,
+        scratch_shapes=[pltpu.VMEM((rows, width), BF16)] * 2 + [pltpu.SemaphoreType.DMA((2 * width // step,))],
         compiler_params=params(),
         name="last",
-    )(far(gk), far(gv), k, v, s)
+    )(gk, gv, k, v, s)
 
 
 def body(queries, keys, values, gain, cotangent):
@@ -350,8 +359,8 @@
     gain = gain.reshape(1, width)
     parts = (count, width // count, DH)
 
-    local = exchange(outer(keys, values, 256).reshape(parts), "ctx")
-    a = within(queries, keys, values)
+    local = exchange(outer(keys, values, 128).reshape(parts), "ctx")
+    a = within(queries, keys, values, 256)
     local, a, gain = lax.optimization_barrier((local, a, gain))
     state = exchange(scan(local, False), "ctx").reshape(width, DH)
 

time: 95.8 us -> 91.5 us (0.955)
  Pallas kernels: 25 us -> 19.2 us
  waiting for transfers between devices: 7.67 us -> 10.7 us
  blocking collectives: 43.9 us -> 42.5 us
    pallas_call x3, Pallas kernels: 10.9 us -> 7.11 us  [the longest x1 4.43 us: within(): pl.pallas_call(functools.partial(within_kernel, step=step), in_specs=[HBM...]
    all_to_all x2, waiting for transfers between devices: 7.67 us -> 10.7 us  [exchange(): return lax.all_to_all(x, axis, 0, 0)]
    pallas_call x1, Pallas kernels: 9.36 us -> 7.54 us  [side(): pl.pallas_call(functools.partial(side_kernel, step=step), in_specs=[HBM]...]
    all_to_all x3, blocking collectives: 43.9 us -> 42.5 us  [exchange(): return lax.all_to_all(x, axis, 0, 0)]
  transfers between devices with their start and end apart: 2 -> 2, of which waited for: 2 -> 2; matrix products, arithmetic and copies ran while one was open for 0% -> 0% of each run, Pallas kernels for 16% -> 13%
where the time goes in v3:
time: 91.5 us; the launch traced here: 90.6 us
  blocking collectives  42.5 us (46%)
  Pallas kernels  19.2 us (21%)
  starting transfers between devices  17.4 us (19%)
  waiting for transfers between devices  10.7 us (12%)
    all_to_all x3, blocking collectives, exchange(): return lax.all_to_all(x, axis, 0, 0)  42.5 us
    all_to_all x2, starting transfers between devices, exchange(): return lax.all_to_all(x, axis, 0, 0)  17.4 us
    all_to_all x2, waiting for transfers between devices, exchange(): return lax.all_to_all(x, axis, 0, 0)  10.7 us
    pallas_call x1, Pallas kernels, side(): pl.pallas_call(functools.partial(side_kernel, step=step), in_specs=[HBM]...  7.54 us
    pallas_call x1, Pallas kernels, within(): pl.pallas_call(functools.partial(within_kernel, step=step), in_specs=[HBM...  4.43 us
    pallas_call x1, Pallas kernels, outer(): pl.pallas_call(functools.partial(outer_kernel, step=step), in_specs=[HBM]...  2.55 us
    pallas_call x1, Pallas kernels, grad(): pl.pallas_call(functools.partial(grad_kernel, total=total), out_specs=[HB...  1.94 us
  transfers between devices with their start and end apart: 2, of which 2 were waited for; matrix products, arithmetic and copies ran while one was open for 0% of the time, Pallas kernels for 13%

profile of v3, /device:TPU:2, one launch (start us, length us, event | category | flops | bytes accessed | tf_op | source)
XLA Modules:
  0.0 90.6 jit_solution(11183579010428686493)
XLA Ops:
  0.6 0.0 copy-start.8
  0.6 2.6 %outer.1 = bf16[1024,128]{1,0:T(8,128)(2,1)} custom-call(bf16[512,1024]{1,0:T(8,128)(2,1)} %k_ref.1, bf16[512,1024]{1,0:T(8,128)(2,1)} %v_ref.1), custom_call_target="tpu_custom_call" | custom-call | tf_op jit(solution)/shard_map/outer/pallas_call | solution.py:86
  3.2 11.6 %all-to-all-start = ((bf16[32,32,128]{2,1,0:T(8,128)(2,1)}), bf16[32,32,128]{2,1,0:T(8,128)(2,1)S(1)}, u32[]{:S(2)}, u32[]{:S(2)}) async-start(bf16[32,32,128]{2,1,0:T(8,128)(2,1)} %bitcast.7), calls=%async_computation | async-start | bytes 524288 | tf_op jit(solution)/shard_map/all_to_all | solution.py:123
  14.8 0.0 copy-done.8
  14.9 4.4 %within.1.a_ref = f32[512,1024]{1,0:T(8,128)} custom-call(bf16[512,1024]{1,0:T(8,128)(2,1)} %q_hbm.3, bf16[512,1024]{1,0:T(8,128)(2,1)} %k_ref.1, bf16[512,1024]{1,0:T(8,128)(2,1)} %v_ref.1), custom_call_target="tpu_custom_call" | custom-call | tf_op jit(solution)/shard_map/within/pallas_call | solution.py:199
  19.3 0.0 copy-start
  19.3 0.0 copy-start.3
  19.3 6.7 %all-to-all-done.x_ref = bf16[32,32,128]{2,1,0:T(8,128)(2,1)S(1)} async-done(((bf16[32,32,128]{2,1,0:T(8,128)(2,1)}), bf16[32,32,128]{2,1,0:T(8,128)(2,1)S(1)}, u32[]{:S(2)}, u32[]{:S(2)}) %all-to-all-start) | async-done | bytes 262176 | tf_op jit(solution)/shard_map/all_to_all | solution.py:123
  26.0 0.0 copy-start.4
  26.1 15.9 %all_to_all.25 = bf16[32,32,128]{2,1,0:T(8,128)(2,1)S(1)} all-to-all(bf16[32,32,128]{2,1,0:T(8,128)(2,1)S(1)} %prefix.1), channel_id=1, replica_groups=mesh['ctx'=32,'head'=8] {'ctx'}, dimensions={0} | all-to-all | bytes 524288 | tf_op jit(solution)/shard_map/all_to_all | solution.py:123
  42.0 0.0 copy-start.5
  42.0 0.0 copy-done
  42.0 0.0 copy-done.3
  42.0 0.0 copy-done.4
  42.0 0.9 attend.1
  42.9 0.0 copy-done.5
  42.9 9.7 %all_to_all.26.stat_ref = f32[8,8,128]{2,1,0:T(8,128)S(1)} all-to-all(f32[8,8,128]{2,1,0:T(8,128)S(1)} %get-tuple-element.25), channel_id=1, replica_groups=mesh['ctx'=32,'head'=8] {'head'}, dimensions={0} | all-to-all | bytes 65536 | tf_op jit(solution)/shard_map/all_to_all | solution.py:123
  52.6 1.9 %grad.1 = (bf16[512,1024]{1,0:T(8,128)(2,1)}, bf16[1024,128]{1,0:T(8,128)(2,1)}, bf16[512,1024]{1,0:T(8,128)(2,1)}) custom-call(f32[512,1024]{1,0:T(8,128)S(1)} %get-tuple-element.24.att_ref, bf16[512,1024]{1,0:T(8,128)(2,1)S(1)} %copy-done.4, bf16[1,1024]{1,0:T(2,128)(2,1)S(1)} %reshape.24.gain_ref, f32[8,8,128]{2,1,0:T(8,128)S(1)} %all_to_all.26.stat_ref, ...), custom_call_target="tpu_custom_call" | custom-call | tf_op jit(solution)/shard_map/grad/pallas_call | solution.py:274
  54.6 5.8 %all-to-all-start.3 = ((bf16[32,32,128]{2,1,0:T(8,128)(2,1)}), bf16[32,32,128]{2,1,0:T(8,128)(2,1)S(1)}, u32[]{:S(2)}, u32[]{:S(2)}) async-start(bf16[32,32,128]{2,1,0:T(8,128)(2,1)} %bitcast.8), calls=%async_computation.3 | async-start | bytes 524288 | tf_op jit(solution)/shard_map/all_to_all | solution.py:123
  60.4 7.5 %side.1 = (bf16[512,1024]{1,0:T(8,128)(2,1)}, f32[512,1024]{1,0:T(8,128)}, f32[512,1024]{1,0:T(8,128)}) custom-call(bf16[512,1024]{1,0:T(8,128)(2,1)} %q_hbm.3, bf16[512,1024]{1,0:T(8,128)(2,1)} %k_ref.1, bf16[512,1024]{1,0:T(8,128)(2,1)} %v_ref.1, bf16[512,1024]{1,0:T(8,128)(2,1)} %get-tuple-element.28.g_hbm, bf16[1024,128]{1,0:T(8,128)(2,1)} %bitcast.5), custom_call_target="tpu_custom_call" | custom-call | tf_op jit(solution)/shard_map/side/pallas_call | solution.py:318
  67.9 4.0 %all-to-all-done.3.x_ref = bf16[32,32,128]{2,1,0:T(8,128)(2,1)S(1)} async-done(((bf16[32,32,128]{2,1,0:T(8,128)(2,1)}), bf16[32,32,128]{2,1,0:T(8,128)(2,1)S(1)}, u32[]{:S(2)}, u32[]{:S(2)}) %all-to-all-start.3) | async-done | bytes 262176 | tf_op jit(solution)/shard_map/all_to_all | solution.py:123
  71.9 0.0 copy-start.1
  71.9 0.0 copy-start.2
  71.9 0.0 copy-start.6
  71.9 0.0 copy-start.7
  71.9 16.9 %all_to_all.27 = bf16[32,32,128]{2,1,0:T(8,128)(2,1)S(1)} all-to-all(bf16[32,32,128]{2,1,0:T(8,128)(2,1)S(1)} %suffix.1), channel_id=1, replica_groups=mesh['ctx'=32,'head'=8] {'ctx'}, dimensions={0} | all-to-all | bytes 524288 | tf_op jit(solution)/shard_map/all_to_all | solution.py:123
  88.8 0.0 copy-done.1
  88.8 0.0 copy-done.2
  88.8 0.0 copy-done.6
  88.8 0.0 copy-done.7
  88.9 1.8 %last.1 = (bf16[512,1024]{1,0:T(8,128)(2,1)}, bf16[512,1024]{1,0:T(8,128)(2,1)}) custom-call(f32[512,1024]{1,0:T(8,128)S(1)} %copy-done.6, f32[512,1024]{1,0:T(8,128)S(1)} %copy-done.7, bf16[512,1024]{1,0:T(8,128)(2,1)S(1)} %copy-done.1, bf16[512,1024]{1,0:T(8,128)(2,1)S(1)} %copy-done.2, bf16[1024,128]{1,0:T(8,128)(2,1)S(1)} %bitcast.6), custom_call_target="tpu_custom_call" | custom-call | tf_op jit(solution)/shard_map/last/pallas_call | solution.py:346
  (3 shorter events, 0.1 us)
Async XLA Ops:
  0.6 14.2 %copy-start.8 = (bf16[1024]{0:T(1024)(128)(2,1)S(1)}, bf16[1024]{0:T(1024)(128)(2,1)}, u32[]{:S(2)}) copy-start(bf16[1024]{0:T(1024)(128)(2,1)} %param.8) | copy-start | bytes 6148
  3.2 22.8 %all-to-all-start = ((bf16[32,32,128]{2,1,0:T(8,128)(2,1)}), bf16[32,32,128]{2,1,0:T(8,128)(2,1)S(1)}, u32[]{:S(2)}, u32[]{:S(2)}) async-start(bf16[32,32,128]{2,1,0:T(8,128)(2,1)} %bitcast.7), calls=%async_computation | async-start | bytes 524288 | tf_op jit(solution)/shard_map/all_to_all | solution.py:123
  19.3 22.7 %copy-start = (bf16[512,1024]{1,0:T(8,128)(2,1)S(1)}, bf16[512,1024]{1,0:T(8,128)(2,1)}, u32[]{:S(2)}) copy-start(bf16[512,1024]{1,0:T(8,128)(2,1)} %q_hbm.3) | copy-start | bytes 3145732
  19.3 22.7 %copy-start.3 = (f32[512,1024]{1,0:T(8,128)S(1)}, f32[512,1024]{1,0:T(8,128)}, u32[]{:S(2)}) copy-start(f32[512,1024]{1,0:T(8,128)} %within.1.a_ref) | copy-start | bytes 6291460
  26.0 15.9 %copy-start.4 = (bf16[512,1024]{1,0:T(8,128)(2,1)S(1)}, bf16[512,1024]{1,0:T(8,128)(2,1)}, u32[]{:S(2)}) copy-start(bf16[512,1024]{1,0:T(8,128)(2,1)} %cot_ref.3) | copy-start | bytes 3145732
  42.0 0.9 %copy-start.5 = (bf16[32,32,128]{2,1,0:T(8,128)(2,1)}, bf16[32,32,128]{2,1,0:T(8,128)(2,1)S(1)}, u32[]{:S(2)}) copy-start(bf16[32,32,128]{2,1,0:T(8,128)(2,1)S(1)} %all_to_all.25) | copy-start | bytes 786436
  54.6 17.3 %all-to-all-start.3 = ((bf16[32,32,128]{2,1,0:T(8,128)(2,1)}), bf16[32,32,128]{2,1,0:T(8,128)(2,1)S(1)}, u32[]{:S(2)}, u32[]{:S(2)}) async-start(bf16[32,32,128]{2,1,0:T(8,128)(2,1)} %bitcast.8), calls=%async_computation.3 | async-start | bytes 524288 | tf_op jit(solution)/shard_map/all_to_all | solution.py:123
  71.9 17.0 %copy-start.1 = (bf16[512,1024]{1,0:T(8,128)(2,1)S(1)}, bf16[512,1024]{1,0:T(8,128)(2,1)}, u32[]{:S(2)}) copy-start(bf16[512,1024]{1,0:T(8,128)(2,1)} %k_ref.1) | copy-start | bytes 3145732
  71.9 17.0 %copy-start.2 = (bf16[512,1024]{1,0:T(8,128)(2,1)S(1)}, bf16[512,1024]{1,0:T(8,128)(2,1)}, u32[]{:S(2)}) copy-start(bf16[512,1024]{1,0:T(8,128)(2,1)} %v_ref.1) | copy-start | bytes 3145732
  71.9 17.0 %copy-start.6 = (f32[512,1024]{1,0:T(8,128)S(1)}, f32[512,1024]{1,0:T(8,128)}, u32[]{:S(2)}) copy-start(f32[512,1024]{1,0:T(8,128)} %get-tuple-element.33.gk_ref) | copy-start | bytes 6291460
  71.9 17.0 %copy-start.7 = (f32[512,1024]{1,0:T(8,128)S(1)}, f32[512,1024]{1,0:T(8,128)}, u32[]{:S(2)}) copy-start(f32[512,1024]{1,0:T(8,128)} %get-tuple-element.34.gv_ref) | copy-start | bytes 6291460

commit v4 on v3

--- a/solution.py
+++ b/solution.py
@@ -11,6 +11,7 @@
 F32 = jnp.float32
 BF16 = jnp.bfloat16
 PART = F32
+FIRST = 18
 SCAN_COST = 10_000_000_000
 VMEM_LIMIT = 16 * 1024 * 1024
 VMEM_MOST = 60 * 1024 * 1024
@@ -67,18 +68,23 @@
     loads = [
         (mover.start(a_hbm.at[rows], a_ref.at[rows]), mover.start(b_hbm.at[rows], b_ref.at[rows])) for rows in chunks
     ]
+    stores = []
     for i, rows in enumerate(chunks):
         for copy in loads[i]:
             copy.wait()
-        for cols in heads_of(a_ref):
+        for h, cols in enumerate(heads_of(a_ref)):
             term = dot(a_ref[rows, cols], b_ref[rows, cols], TN)
             if i > 0:
                 term = acc_ref[cols, :] + term
             if i < len(chunks) - 1:
                 acc_ref[cols, :] = term
-            else:
-                out_ref[cols, :] = term.astype(BF16)
-    mover.start(out_ref, out_hbm).wait()
+                continue
+            out_ref[cols, :] = term.astype(BF16)
+            if h % 4 == 3:
+                four = slice(cols.stop - 4 * DH, cols.stop)
+                stores.append(mover.start(out_ref.at[four], out_hbm.at[four]))
+    for copy in stores:
+        copy.wait()
 
 
 def outer(a, b, step):
@@ -93,18 +99,23 @@
             pltpu.VMEM((rows, width), BF16),
             pltpu.VMEM((width, DH), F32),
             pltpu.VMEM((width, DH), BF16),
-            pltpu.SemaphoreType.DMA((2 * rows // step + 1,)),
+            pltpu.SemaphoreType.DMA((2 * rows // step + width // DH // 4,)),
         ],
         compiler_params=params(VMEM_MOST),
         name="outer",
     )(far(a), far(b))
 
 
+def ring(count, first):
+    return [(first + i) % count for i in range(count)]
+
+
 def scan_kernel(x_ref, out_ref, *, backward):
     count = x_ref.shape[0]
     total = jnp.zeros(x_ref.shape[1:], F32)
+    place = {block: i for i, block in enumerate(ring(count, FIRST))}
     for lap in range(count):
-        i = count - 1 - lap if backward else lap
+        i = place[count - 1 - lap if backward else lap]
         out_ref[i] = total.astype(BF16)
         total = total + x_ref[i].astype(F32)
 
@@ -120,7 +131,14 @@
 
 
 def exchange(x, axis):
-    return lax.all_to_all(x, axis, 0, 0)
+    return lax.all_to_all(x, axis, 0, 0, axis_index_groups=[ring(x.shape[0], FIRST)])
+
+
+def gathered(x, axis):
+    count = lax.axis_size(axis)
+    pair = x + lax.ppermute(x, axis, [(i, i ^ 1) for i in range(count)])
+    steps = range(2, count, 2)
+    return [pair, *(lax.ppermute(pair, axis, [(i, (i + d) % count) for i in range(count)]) for d in steps)]
 
 
 def keep_lower(x):
@@ -207,46 +225,51 @@
     )(far(q), far(k), far(v))
 
 
-def attend_kernel(a_ref, q_ref, s_ref, cot_ref, gain_ref, att_ref, stat_ref, sum_ref):
+def side_by_side(one, two):
+    return jnp.concatenate(
+        [
+            jnp.concatenate([one, jnp.zeros_like(two)], axis=1),
+            jnp.concatenate([jnp.zeros_like(one), two], axis=1),
+        ],
+        axis=0,
+    )
+
+
+def attend_kernel(a_ref, q_ref, s_ref, cot_ref, gain_ref, att_ref, stat_ref, sq_ref, cr_ref):
+    for i, pair in enumerate(groups_of(q_ref, 2 * DH)):
+        s = side_by_side(s_ref[pair.start : pair.start + DH, :], s_ref[pair.start + DH : pair.stop, :])
+        att = a_ref[:, pair] + dot(q_ref[:, pair], s, NN)
+        att_ref[:, pair] = att
+        scaled = cot_ref[:, pair].astype(F32) * gain_ref[:, pair].astype(F32)
+        for ref, term in ((sq_ref, att * att), (cr_ref, scaled * att)):
+            term = term[:, :DH] + term[:, DH:]
+            ref[...] = term if i == 0 else ref[...] + term
     chunks = chunks_of(q_ref, DH)
-    for i, span in enumerate(chunks):
-        sq = jnp.zeros((DH, DH), F32)
-        cr = jnp.zeros((DH, DH), F32)
-        for cols in heads_of(q_ref):
-            att = a_ref[span, cols] + dot(q_ref[span, cols], s_ref[cols, :], NN)
-            att_ref[span, cols] = att
-            scaled = cot_ref[span, cols].astype(F32) * gain_ref[:, cols].astype(F32)
-            sq += att * att
-            cr += scaled * att
-        sum_ref[i] = sq
-        sum_ref[len(chunks) + i] = cr
-    lines = [jnp.sum(sum_ref[i].T, axis=0, keepdims=True) for i in range(sum_ref.shape[0])]
-    lines = jnp.concatenate(lines, axis=0)
-    for copy in range(stat_ref.shape[0]):
-        stat_ref[copy] = lines
-
-
-def attend(a, q, s, cot, gain, copies):
+    lines = [jnp.sum(ref[span, :].T, axis=0, keepdims=True) for ref in (sq_ref, cr_ref) for span in chunks]
+    stat_ref[...] = jnp.concatenate(lines, axis=0)
+
+
+def attend(a, q, s, cot, gain):
     rows, width = q.shape
     return pl.pallas_call(
         attend_kernel,
         out_shape=[
             jax.ShapeDtypeStruct((rows, width), F32),
-            jax.ShapeDtypeStruct((copies, 2 * rows // DH, DH), F32),
+            jax.ShapeDtypeStruct((2 * rows // DH, DH), F32),
         ],
-        scratch_shapes=[pltpu.VMEM((2 * rows // DH, DH, DH), F32)],
+        scratch_shapes=[pltpu.VMEM((rows, DH), F32)] * 2,
         compiler_params=params(),
         name="attend",
     )(a, q, s, cot, gain)
 
 
 def grad_kernel(
-    att_ref, cot_ref, gain_ref, stat_ref, q_ref, g_hbm, lg_hbm, n_hbm, g_ref, lg_ref, n_ref, sems, *, total
+    att_ref, cot_ref, gain_ref, q_ref, s0_ref, s1_ref, s2_ref, s3_ref, g_hbm, lg_hbm, n_hbm, g_ref, lg_ref, n_ref, sems, *, total
 ):
     mover = Mover(sems)
     rows = att_ref.shape[0]
     blocks = rows // DH
-    stats = jnp.sum(stat_ref[...], axis=0) / total
+    stats = ((s0_ref[...] + s1_ref[...]) + (s2_ref[...] + s3_ref[...])) / total
     inv = lax.rsqrt(stats[:blocks] + 1e-06)
     pull = inv**3 * stats[blocks:]
     stores = []
@@ -279,7 +302,7 @@
         + [pltpu.SemaphoreType.DMA((2 * rows // DH + 1,))],
         compiler_params=params(),
         name="grad",
-    )(att, cot, gain, stats, q)
+    )(att, cot, gain, q, *stats)
 
 
 def side_kernel(q_hbm, k_hbm, v_hbm, g_hbm, s_hbm, *refs, step):
@@ -287,7 +310,7 @@
     mover = Mover(sems)
     half = q_ref.shape[0] // 2
     groups = groups_of(q_ref, step)
-    here = step // DH
+    many = step // DH
     s_in = mover.start(s_hbm, s_ref)
     pairs = ((g_hbm, g_ref), (v_hbm, v_ref), (k_hbm, k_ref), (q_hbm, q_ref))
     loads = [[mover.start(src.at[:, group], dst.at[:, group]) for src, dst in pairs] for group in groups]
@@ -296,15 +319,19 @@
     for i, group in enumerate(groups):
         for copy in loads[i]:
             copy.wait()
-        spans = heads_of(q_ref)[i * here : (i + 1) * here]
-        for cols in spans:
+        spans = heads_of(q_ref)[i * many : (i + 1) * many]
+        for j, cols in enumerate(spans):
+            if j % 2 == 0:
+                span = slice(cols.start, cols.start + 2 * DH)
+                s = side_by_side(s_ref[cols, :].T, s_ref[cols.stop : span.stop, :].T)
+                rest = dot(g_ref[:, span], s, NN)
+            here = slice(j % 2 * DH, (j % 2 + 1) * DH)
             q, k, v, g = q_ref[:, cols], k_ref[:, cols], v_ref[:, cols], g_ref[:, cols]
             pull = upper_parts(v, g)
             attn = upper_parts(k, q)
-            rest = dot(g, s_ref[cols, :], NT)
             put(gk_ref, cols, upper_apply(pull, q))
             one, two = upper_turned(pull, k)
-            put(gq_ref, cols, (one + rest[:half], two + rest[half:]))
+            put(gq_ref, cols, (one + rest[:half, here], two + rest[half:, here]))
             put(gv_ref, cols, upper_apply(attn, g))
         for src, dst in ((gk_ref, gk_hbm), (gv_ref, gv_hbm), (gq_ref, gq_hbm)):
             stores.append(mover.start(src.at[:, group], dst.at[:, group]))
@@ -333,8 +360,9 @@
     for group in groups_of(k_ref, step):
         for cols in heads_of(k_ref)[group.start // DH : group.stop // DH]:
             s = s_ref[cols, :]
-            outk_ref[:, cols] = (gk_ref[:, cols] + dot(v_ref[:, cols], s, NT)).astype(BF16)
-            outv_ref[:, cols] = (gv_ref[:, cols] + dot(k_ref[:, cols], s, NN)).astype(BF16)
+            both = dot(jnp.concatenate([v_ref[:, cols], k_ref[:, cols]], axis=1), side_by_side(s.T, s), NN)
+            outk_ref[:, cols] = (gk_ref[:, cols] + both[:, :DH]).astype(BF16)
+            outv_ref[:, cols] = (gv_ref[:, cols] + both[:, DH:]).astype(BF16)
         stores.append(mover.start(outk_ref.at[:, group], outk_hbm.at[:, group]))
         stores.append(mover.start(outv_ref.at[:, group], outv_hbm.at[:, group]))
     for copy in stores:
@@ -364,8 +392,8 @@
     local, a, gain = lax.optimization_barrier((local, a, gain))
     state = exchange(scan(local, False), "ctx").reshape(width, DH)
 
-    att, stats = attend(a, queries, state, cotangent, gain, heads)
-    stats = exchange(stats, "head")
+    att, stats = attend(a, queries, state, cotangent, gain)
+    stats = gathered(stats, "head")
     g, local, normed = grad(att, cotangent, gain, stats, queries, width * heads)
 
     local = exchange(local.reshape(parts), "ctx")

time: 91.5 us -> 86.9 us (0.950)
  blocking collectives: 42.5 us -> 32 us
  starting transfers between devices: 17.4 us -> 26.3 us
  waiting for transfers between devices: 10.7 us -> 8 us
    all_to_all x3 -> x2, blocking collectives: 42.5 us -> 32 us  [exchange(): lax.all_to_all(x, axis, 0, 0, axis_index_groups=[ring(x.shape[0], FIRST)])]
    all_to_all x2, waiting for transfers between devices: 10.7 us -> 3 us  [exchange(): lax.all_to_all(x, axis, 0, 0, axis_index_groups=[ring(x.shape[0], FIRST)])]
    ppermute x0 -> x4, waiting for transfers between devices: none -> 5 us  [the longest x3 3.84 us: gathered(): lax.ppermute(pair, axis, [(i, (i + d) % count) for i in range(count)])]
    ppermute x0 -> x4, starting transfers between devices: none -> 4.71 us  [the longest x3 4.61 us: gathered(): lax.ppermute(pair, axis, [(i, (i + d) % count) for i in range(count)])]
    all_to_all x2, starting transfers between devices: 17.4 us -> 21.6 us  [exchange(): lax.all_to_all(x, axis, 0, 0, axis_index_groups=[ring(x.shape[0], FIRST)])]
  transfers between devices with their start and end apart: 2 -> 6, of which waited for: 2 -> 4; matrix products, arithmetic and copies ran while one was open for 0% -> 0% of each run, Pallas kernels for 13% -> 14%
where the time goes in v4:
time: 86.9 us; the launch traced here: 86.5 us
  blocking collectives  32 us (37%)
  starting transfers between devices  26.3 us (30%)
  Pallas kernels  19.2 us (22%)
  waiting for transfers between devices  8 us (9%)
  between operations  0.97 us (1%)
    all_to_all x2, blocking collectives, exchange(): lax.all_to_all(x, axis, 0, 0, axis_index_groups=[ring(x.shape[0], FIRST)])  32 us
    all_to_all x2, starting transfers between devices, exchange(): lax.all_to_all(x, axis, 0, 0, axis_index_groups=[ring(x.shape[0], FIRST)])  21.6 us
    pallas_call x1, Pallas kernels, side(): pl.pallas_call(functools.partial(side_kernel, step=step), in_specs=[HBM]...  7.66 us
    ppermute x3, starting transfers between devices, gathered(): lax.ppermute(pair, axis, [(i, (i + d) % count) for i in range(count)])  4.61 us
    pallas_call x1, Pallas kernels, within(): pl.pallas_call(functools.partial(within_kernel, step=step), in_specs=[HBM...  4.44 us
    ppermute x3, waiting for transfers between devices, gathered(): lax.ppermute(pair, axis, [(i, (i + d) % count) for i in range(count)])  3.84 us
    all_to_all x2, waiting for transfers between devices, exchange(): lax.all_to_all(x, axis, 0, 0, axis_index_groups=[ring(x.shape[0], FIRST)])  3 us
    pallas_call x1, Pallas kernels, outer(): pl.pallas_call(functools.partial(outer_kernel, step=step), in_specs=[HBM]...  2.51 us
  transfers between devices with their start and end apart: 6, of which 4 were waited for; matrix products, arithmetic and copies ran while one was open for 0% of the time, Pallas kernels for 14%

profile of v4, /device:TPU:2, one launch (start us, length us, event | category | flops | bytes accessed | tf_op | source)
XLA Modules:
  0.0 86.5 jit_solution(11159566363756443272)
XLA Ops:
  0.6 0.0 copy-start.8
  0.6 2.5 %outer.1 = bf16[1024,128]{1,0:T(8,128)(2,1)} custom-call(bf16[512,1024]{1,0:T(8,128)(2,1)} %k_ref.1, bf16[512,1024]{1,0:T(8,128)(2,1)} %v_ref.1), custom_call_target="tpu_custom_call" | custom-call | tf_op jit(solution)/shard_map/outer/pallas_call | solution.py:92
  3.2 12.1 %all-to-all-start = ((bf16[32,32,128]{2,1,0:T(8,128)(2,1)}), bf16[32,32,128]{2,1,0:T(8,128)(2,1)S(1)}, u32[]{:S(2)}, u32[]{:S(2)}) async-start(bf16[32,32,128]{2,1,0:T(8,128)(2,1)} %bitcast.7), calls=%async_computation | async-start | bytes 524288 | tf_op jit(solution)/shard_map/all_to_all | solution.py:134
  15.3 0.0 copy-done.8
  15.3 4.4 %within.1.a_ref = f32[512,1024]{1,0:T(8,128)} custom-call(bf16[512,1024]{1,0:T(8,128)(2,1)} %q_hbm.3, bf16[512,1024]{1,0:T(8,128)(2,1)} %k_ref.1, bf16[512,1024]{1,0:T(8,128)(2,1)} %v_ref.1), custom_call_target="tpu_custom_call" | custom-call | tf_op jit(solution)/shard_map/within/pallas_call | solution.py:217
  19.8 0.0 copy-start
  19.8 0.0 copy-start.3
  19.8 3.0 %all-to-all-done.x_ref = bf16[32,32,128]{2,1,0:T(8,128)(2,1)S(1)} async-done(((bf16[32,32,128]{2,1,0:T(8,128)(2,1)}), bf16[32,32,128]{2,1,0:T(8,128)(2,1)S(1)}, u32[]{:S(2)}, u32[]{:S(2)}) %all-to-all-start) | async-done | bytes 262176 | tf_op jit(solution)/shard_map/all_to_all | solution.py:134
  22.8 0.0 copy-start.4
  22.8 15.9 %all_to_all.20 = bf16[32,32,128]{2,1,0:T(8,128)(2,1)S(1)} all-to-all(bf16[32,32,128]{2,1,0:T(8,128)(2,1)S(1)} %prefix.1), channel_id=1, replica_groups={{144,152,160,168,176,184,192,200,208,216,224,232,240,248,0,8,16,24,32,4..., dimensions={0} | all-to-all | bytes 524288 | tf_op jit(solution)/shard_map/all_to_all | solution.py:134
  38.7 0.0 copy-start.5
  38.7 0.0 copy-done
  38.7 0.0 copy-done.3
  38.7 0.0 copy-done.4
  38.7 0.8 attend.1
  39.5 0.0 copy-done.5
  39.6 0.1 collective-permute-start
  39.7 1.2 %collective-permute-done = f32[8,128]{1,0:T(8,128)S(1)} collective-permute-done((f32[8,128]{1,0:T(8,128)S(1)}, f32[8,128]{1,0:T(8,128)S(1)}, u32[]{:S(2)}, u32[]{:S(2)}) %collective-permute-start) | collective-permute-done | bytes 4128 | tf_op jit(solution)/shard_map/ppermute | solution.py:139
  40.8 3.0 %collective-permute-start.3 = (f32[8,128]{1,0:T(8,128)S(1)}, f32[8,128]{1,0:T(8,128)S(1)}, u32[]{:S(2)}, u32[]{:S(2)}) collective-permute-start(f32[8,128]{1,0:T(8,128)S(1)} %add.3.s0_ref), channel_id=1, source_target_pairs={{0,6},{1,7},{2,0},{3,1},{4,2},{5,3},{6,4},{7,5},{8,14},{9,15},{10,... | collective-permute-start | bytes 12296 | tf_op jit(solution)/shard_map/ppermute | solution.py:141
  43.8 0.6 collective-permute-start.2
  44.5 1.0 %collective-permute-start.1 = (f32[8,128]{1,0:T(8,128)S(1)}, f32[8,128]{1,0:T(8,128)S(1)}, u32[]{:S(2)}, u32[]{:S(2)}) collective-permute-start(f32[8,128]{1,0:T(8,128)S(1)} %add.3.s0_ref), channel_id=1, source_target_pairs={{0,2},{1,3},{2,4},{3,5},{4,6},{5,7},{6,0},{7,1},{8,10},{9,11},{10,... | collective-permute-start | bytes 12296 | tf_op jit(solution)/shard_map/ppermute | solution.py:141
  45.4 0.0 collective-permute-done.3.s3_ref
  45.4 3.5 %collective-permute-done.2.s2_ref = f32[8,128]{1,0:T(8,128)S(1)} collective-permute-done((f32[8,128]{1,0:T(8,128)S(1)}, f32[8,128]{1,0:T(8,128)S(1)}, u32[]{:S(2)}, u32[]{:S(2)}) %collective-permute-start.2) | collective-permute-done | bytes 4128 | tf_op jit(solution)/shard_map/ppermute | solution.py:141
  48.9 0.3 collective-permute-done.1.s1_ref
  49.3 1.9 %grad.1 = (bf16[512,1024]{1,0:T(8,128)(2,1)}, bf16[1024,128]{1,0:T(8,128)(2,1)}, bf16[512,1024]{1,0:T(8,128)(2,1)}) custom-call(f32[512,1024]{1,0:T(8,128)S(1)} %get-tuple-element.24.att_ref, bf16[512,1024]{1,0:T(8,128)(2,1)S(1)} %copy-done.4, bf16[1,1024]{1,0:T(2,128)(2,1)S(1)} %reshape.24.gain_ref, bf16[512,1024]{1,0:T(8,128)(2,1)S(1)} %copy-done, ...), custom_call_target="tpu_custom_call" | custom-call | tf_op jit(solution)/shard_map/grad/pallas_call | solution.py:297
  51.2 9.4 %all-to-all-start.2 = ((bf16[32,32,128]{2,1,0:T(8,128)(2,1)}), bf16[32,32,128]{2,1,0:T(8,128)(2,1)S(1)}, u32[]{:S(2)}, u32[]{:S(2)}) async-start(bf16[32,32,128]{2,1,0:T(8,128)(2,1)} %bitcast.8), calls=%async_computation.2 | async-start | bytes 524288 | tf_op jit(solution)/shard_map/all_to_all | solution.py:134
  60.7 7.7 %side.1 = (bf16[512,1024]{1,0:T(8,128)(2,1)}, f32[512,1024]{1,0:T(8,128)}, f32[512,1024]{1,0:T(8,128)}) custom-call(bf16[512,1024]{1,0:T(8,128)(2,1)} %q_hbm.3, bf16[512,1024]{1,0:T(8,128)(2,1)} %k_ref.1, bf16[512,1024]{1,0:T(8,128)(2,1)} %v_ref.1, bf16[512,1024]{1,0:T(8,128)(2,1)} %get-tuple-element.28.g_hbm, bf16[1024,128]{1,0:T(8,128)(2,1)} %bitcast.5), custom_call_target="tpu_custom_call" | custom-call | tf_op jit(solution)/shard_map/side/pallas_call | solution.py:345
  68.3 0.0 all-to-all-done.2.x_ref
  68.4 0.0 copy-start.1
  68.4 0.0 copy-start.2
  68.4 0.0 copy-start.6
  68.4 0.0 copy-start.7
  68.4 16.1 %all_to_all.21 = bf16[32,32,128]{2,1,0:T(8,128)(2,1)S(1)} all-to-all(bf16[32,32,128]{2,1,0:T(8,128)(2,1)S(1)} %suffix.1), channel_id=1, replica_groups={{144,152,160,168,176,184,192,200,208,216,224,232,240,248,0,8,16,24,32,4..., dimensions={0} | all-to-all | bytes 524288 | tf_op jit(solution)/shard_map/all_to_all | solution.py:134
  84.6 0.0 copy-done.1
  84.6 0.0 copy-done.2
  84.6 0.0 copy-done.6
  84.6 0.0 copy-done.7
  84.6 1.7 %last.1 = (bf16[512,1024]{1,0:T(8,128)(2,1)}, bf16[512,1024]{1,0:T(8,128)(2,1)}) custom-call(f32[512,1024]{1,0:T(8,128)S(1)} %copy-done.6, f32[512,1024]{1,0:T(8,128)S(1)} %copy-done.7, bf16[512,1024]{1,0:T(8,128)(2,1)S(1)} %copy-done.1, bf16[512,1024]{1,0:T(8,128)(2,1)S(1)} %copy-done.2, bf16[1024,128]{1,0:T(8,128)(2,1)S(1)} %bitcast.6), custom_call_target="tpu_custom_call" | custom-call | tf_op jit(solution)/shard_map/last/pallas_call | solution.py:374
  (4 shorter events, 0.1 us)
Async XLA Ops:
  0.6 14.7 %copy-start.8 = (bf16[1024]{0:T(1024)(128)(2,1)S(1)}, bf16[1024]{0:T(1024)(128)(2,1)}, u32[]{:S(2)}) copy-start(bf16[1024]{0:T(1024)(128)(2,1)} %param.8) | copy-start | bytes 6148
  3.2 19.6 %all-to-all-start = ((bf16[32,32,128]{2,1,0:T(8,128)(2,1)}), bf16[32,32,128]{2,1,0:T(8,128)(2,1)S(1)}, u32[]{:S(2)}, u32[]{:S(2)}) async-start(bf16[32,32,128]{2,1,0:T(8,128)(2,1)} %bitcast.7), calls=%async_computation | async-start | bytes 524288 | tf_op jit(solution)/shard_map/all_to_all | solution.py:134
  19.8 18.9 %copy-start = (bf16[512,1024]{1,0:T(8,128)(2,1)S(1)}, bf16[512,1024]{1,0:T(8,128)(2,1)}, u32[]{:S(2)}) copy-start(bf16[512,1024]{1,0:T(8,128)(2,1)} %q_hbm.3) | copy-start | bytes 3145732
  19.8 18.9 %copy-start.3 = (f32[512,1024]{1,0:T(8,128)S(1)}, f32[512,1024]{1,0:T(8,128)}, u32[]{:S(2)}) copy-start(f32[512,1024]{1,0:T(8,128)} %within.1.a_ref) | copy-start | bytes 6291460
  22.8 15.9 %copy-start.4 = (bf16[512,1024]{1,0:T(8,128)(2,1)S(1)}, bf16[512,1024]{1,0:T(8,128)(2,1)}, u32[]{:S(2)}) copy-start(bf16[512,1024]{1,0:T(8,128)(2,1)} %cot_ref.3) | copy-start | bytes 3145732
  38.7 0.8 copy-start.5
  39.6 1.3 %collective-permute-start = (f32[8,128]{1,0:T(8,128)S(1)}, f32[8,128]{1,0:T(8,128)S(1)}, u32[]{:S(2)}, u32[]{:S(2)}) collective-permute-start(f32[8,128]{1,0:T(8,128)S(1)} %get-tuple-element.25), channel_id=1, source_target_pairs={{0,1},{1,0},{2,3},{3,2},{4,5},{5,4},{6,7},{7,6},{8,9},{9,8},{10,11... | collective-permute-start | bytes 12296 | tf_op jit(solution)/shard_map/ppermute | solution.py:139
  40.8 4.6 %collective-permute-start.3 = (f32[8,128]{1,0:T(8,128)S(1)}, f32[8,128]{1,0:T(8,128)S(1)}, u32[]{:S(2)}, u32[]{:S(2)}) collective-permute-start(f32[8,128]{1,0:T(8,128)S(1)} %add.3.s0_ref), channel_id=1, source_target_pairs={{0,6},{1,7},{2,0},{3,1},{4,2},{5,3},{6,4},{7,5},{8,14},{9,15},{10,... | collective-permute-start | bytes 12296 | tf_op jit(solution)/shard_map/ppermute | solution.py:141
  43.8 5.1 %collective-permute-start.2 = (f32[8,128]{1,0:T(8,128)S(1)}, f32[8,128]{1,0:T(8,128)S(1)}, u32[]{:S(2)}, u32[]{:S(2)}) collective-permute-start(f32[8,128]{1,0:T(8,128)S(1)} %add.3.s0_ref), channel_id=1, source_target_pairs={{0,4},{1,5},{2,6},{3,7},{4,0},{5,1},{6,2},{7,3},{8,12},{9,13},{10,... | collective-permute-start | bytes 12296 | tf_op jit(solution)/shard_map/ppermute | solution.py:141
  44.5 4.8 %collective-permute-start.1 = (f32[8,128]{1,0:T(8,128)S(1)}, f32[8,128]{1,0:T(8,128)S(1)}, u32[]{:S(2)}, u32[]{:S(2)}) collective-permute-start(f32[8,128]{1,0:T(8,128)S(1)} %add.3.s0_ref), channel_id=1, source_target_pairs={{0,2},{1,3},{2,4},{3,5},{4,6},{5,7},{6,0},{7,1},{8,10},{9,11},{10,... | collective-permute-start | bytes 12296 | tf_op jit(solution)/shard_map/ppermute | solution.py:141
  51.2 17.1 %all-to-all-start.2 = ((bf16[32,32,128]{2,1,0:T(8,128)(2,1)}), bf16[32,32,128]{2,1,0:T(8,128)(2,1)S(1)}, u32[]{:S(2)}, u32[]{:S(2)}) async-start(bf16[32,32,128]{2,1,0:T(8,128)(2,1)} %bitcast.8), calls=%async_computation.2 | async-start | bytes 524288 | tf_op jit(solution)/shard_map/all_to_all | solution.py:134
  68.4 16.2 %copy-start.1 = (bf16[512,1024]{1,0:T(8,128)(2,1)S(1)}, bf16[512,1024]{1,0:T(8,128)(2,1)}, u32[]{:S(2)}) copy-start(bf16[512,1024]{1,0:T(8,128)(2,1)} %k_ref.1) | copy-start | bytes 3145732
  68.4 16.2 %copy-start.2 = (bf16[512,1024]{1,0:T(8,128)(2,1)S(1)}, bf16[512,1024]{1,0:T(8,128)(2,1)}, u32[]{:S(2)}) copy-start(bf16[512,1024]{1,0:T(8,128)(2,1)} %v_ref.1) | copy-start | bytes 3145732
  68.4 16.2 %copy-start.6 = (f32[512,1024]{1,0:T(8,128)S(1)}, f32[512,1024]{1,0:T(8,128)}, u32[]{:S(2)}) copy-start(f32[512,1024]{1,0:T(8,128)} %get-tuple-element.33.gk_ref) | copy-start | bytes 6291460
  68.4 16.2 %copy-start.7 = (f32[512,1024]{1,0:T(8,128)S(1)}, f32[512,1024]{1,0:T(8,128)}, u32[]{:S(2)}) copy-start(f32[512,1024]{1,0:T(8,128)} %get-tuple-element.34.gv_ref) | copy-start | bytes 6291460

commit v5 on v4

--- a/solution.py
+++ b/solution.py
@@ -15,6 +15,7 @@
 SCAN_COST = 10_000_000_000
 VMEM_LIMIT = 16 * 1024 * 1024
 VMEM_MOST = 60 * 1024 * 1024
+SIDE_VMEM = 24 * 1024 * 1024
 VMEM = pl.BlockSpec(memory_space=pltpu.VMEM)
 
 
@@ -300,38 +301,39 @@
         out_shape=[pltpu.HBM(shape, BF16) for shape in shapes],
         scratch_shapes=[pltpu.VMEM(shape, BF16) for shape in shapes]
         + [pltpu.SemaphoreType.DMA((2 * rows // DH + 1,))],
+        cost_estimate=pl.CostEstimate(flops=SCAN_COST, bytes_accessed=SCAN_COST // 300, transcendentals=0),
         compiler_params=params(),
         name="grad",
     )(att, cot, gain, q, *stats)
 
 
-def side_kernel(q_hbm, k_hbm, v_hbm, g_hbm, s_hbm, *refs, step):
-    gq_hbm, gk_hbm, gv_hbm, q_ref, k_ref, v_ref, g_ref, s_ref, gq_ref, gk_ref, gv_ref, sems = refs
+def side_kernel(q_ref, k_ref, v_hbm, g_hbm, s_hbm, *refs, sizes):
+    gq_hbm, gk_hbm, gv_hbm, v_ref, g_ref, s_ref, gq_ref, gk_ref, gv_ref, sems = refs
     mover = Mover(sems)
     half = q_ref.shape[0] // 2
-    groups = groups_of(q_ref, step)
-    many = step // DH
+    groups = []
+    for size in sizes:
+        start = groups[-1].stop if groups else 0
+        groups.append(slice(start, start + size * DH))
     s_in = mover.start(s_hbm, s_ref)
-    pairs = ((g_hbm, g_ref), (v_hbm, v_ref), (k_hbm, k_ref), (q_hbm, q_ref))
+    pairs = ((g_hbm, g_ref), (v_hbm, v_ref))
     loads = [[mover.start(src.at[:, group], dst.at[:, group]) for src, dst in pairs] for group in groups]
     stores = []
-    s_in.wait()
     for i, group in enumerate(groups):
+        spans = heads_of(q_ref)[group.start // DH : group.stop // DH]
+        if i == 0:
+            first = [upper_parts(k_ref[:, cols], q_ref[:, cols]) for cols in spans]
+            s_in.wait()
         for copy in loads[i]:
             copy.wait()
-        spans = heads_of(q_ref)[i * many : (i + 1) * many]
         for j, cols in enumerate(spans):
-            if j % 2 == 0:
-                span = slice(cols.start, cols.start + 2 * DH)
-                s = side_by_side(s_ref[cols, :].T, s_ref[cols.stop : span.stop, :].T)
-                rest = dot(g_ref[:, span], s, NN)
-            here = slice(j % 2 * DH, (j % 2 + 1) * DH)
             q, k, v, g = q_ref[:, cols], k_ref[:, cols], v_ref[:, cols], g_ref[:, cols]
             pull = upper_parts(v, g)
-            attn = upper_parts(k, q)
+            attn = first[j] if i == 0 else upper_parts(k, q)
+            rest = dot(g, s_ref[cols, :], NT)
             put(gk_ref, cols, upper_apply(pull, q))
             one, two = upper_turned(pull, k)
-            put(gq_ref, cols, (one + rest[:half, here], two + rest[half:, here]))
+            put(gq_ref, cols, (one + rest[:half], two + rest[half:]))
             put(gv_ref, cols, upper_apply(attn, g))
         for src, dst in ((gk_ref, gk_hbm), (gv_ref, gv_hbm), (gq_ref, gq_hbm)):
             stores.append(mover.start(src.at[:, group], dst.at[:, group]))
@@ -339,19 +341,19 @@
         copy.wait()
 
 
-def side(q, k, v, g, s, step):
+def side(q, k, v, g, s, sizes):
     outs = [pltpu.HBM(q.shape, kind) for kind in (BF16, PART, PART)]
     ins = (q, k, v, g, s)
     return pl.pallas_call(
-        functools.partial(side_kernel, step=step),
-        in_specs=[HBM] * len(ins),
+        functools.partial(side_kernel, sizes=sizes),
+        in_specs=[VMEM] * 2 + [HBM] * 3,
         out_specs=[HBM] * len(outs),
         out_shape=outs,
-        scratch_shapes=[pltpu.VMEM(x.shape, x.dtype) for x in (*ins, *outs)]
-        + [pltpu.SemaphoreType.DMA((1 + 7 * q.shape[1] // step,))],
-        compiler_params=params(VMEM_MOST),
+        scratch_shapes=[pltpu.VMEM(x.shape, x.dtype) for x in (*ins[2:], *outs)]
+        + [pltpu.SemaphoreType.DMA((1 + 5 * len(sizes),))],
+        compiler_params=params(SIDE_VMEM),
         name="side",
-    )(*[far(x) for x in ins])
+    )(q, k, *[far(x) for x in ins[2:]])
 
 
 def last_kernel(gk_ref, gv_ref, k_ref, v_ref, s_ref, outk_hbm, outv_hbm, outk_ref, outv_ref, sems, *, step):
@@ -397,7 +399,7 @@
     g, local, normed = grad(att, cotangent, gain, stats, queries, width * heads)
 
     local = exchange(local.reshape(parts), "ctx")
-    sides = side(queries, keys, values, g, state, 256)
+    sides = side(queries, keys, values, g, state, (2, 4, 2))
     local, grad_q, gk, gv = lax.optimization_barrier((local, *sides))
     later = exchange(scan(local, True), "ctx").reshape(width, DH)
     grad_k, grad_v = last(gk, gv, keys, values, later, 256)

time: 86.9 us -> 86.1 us (level)
  transfers between devices with their start and end apart: 6 -> 6, of which waited for: 4 -> 4; matrix products, arithmetic and copies ran while one was open for 0% -> 0% of each run, Pallas kernels for 14% -> 13%
where the time goes in v5:
time: 86.1 us; the launch traced here: 85.8 us
  blocking collectives  32 us (37%)
  starting transfers between devices  26.3 us (31%)
  Pallas kernels  18.5 us (21%)
  waiting for transfers between devices  8 us (9%)
  between operations  0.96 us (1%)
    all_to_all x2, blocking collectives, exchange(): lax.all_to_all(x, axis, 0, 0, axis_index_groups=[ring(x.shape[0], FIRST)])  32 us
    all_to_all x2, starting transfers between devices, exchange(): lax.all_to_all(x, axis, 0, 0, axis_index_groups=[ring(x.shape[0], FIRST)])  21.6 us
    pallas_call x1, Pallas kernels, side(): pl.pallas_call(functools.partial(side_kernel, sizes=sizes), in_specs=[VME...  6.92 us
    ppermute x3, starting transfers between devices, gathered(): lax.ppermute(pair, axis, [(i, (i + d) % count) for i in range(count)])  4.61 us
    pallas_call x1, Pallas kernels, within(): pl.pallas_call(functools.partial(within_kernel, step=step), in_specs=[HBM...  4.44 us
    ppermute x3, waiting for transfers between devices, gathered(): lax.ppermute(pair, axis, [(i, (i + d) % count) for i in range(count)])  3.85 us
    all_to_all x2, waiting for transfers between devices, exchange(): lax.all_to_all(x, axis, 0, 0, axis_index_groups=[ring(x.shape[0], FIRST)])  3 us
    pallas_call x1, Pallas kernels, outer(): pl.pallas_call(functools.partial(outer_kernel, step=step), in_specs=[HBM]...  2.51 us
  transfers between devices with their start and end apart: 6, of which 4 were waited for; matrix products, arithmetic and copies ran while one was open for 0% of the time, Pallas kernels for 13%

profile of v5, /device:TPU:2, one launch (start us, length us, event | category | flops | bytes accessed | tf_op | source)
XLA Modules:
  0.0 85.8 jit_solution(1252508824066404838)
XLA Ops:
  0.6 0.0 copy-start.8
  0.6 2.5 %outer.1 = bf16[1024,128]{1,0:T(8,128)(2,1)} custom-call(bf16[512,1024]{1,0:T(8,128)(2,1)} %k_ref.3, bf16[512,1024]{1,0:T(8,128)(2,1)} %v_ref.1), custom_call_target="tpu_custom_call" | custom-call | tf_op jit(solution)/shard_map/outer/pallas_call | solution.py:93
  3.2 12.1 %all-to-all-start = ((bf16[32,32,128]{2,1,0:T(8,128)(2,1)}), bf16[32,32,128]{2,1,0:T(8,128)(2,1)S(1)}, u32[]{:S(2)}, u32[]{:S(2)}) async-start(bf16[32,32,128]{2,1,0:T(8,128)(2,1)} %bitcast.7), calls=%async_computation | async-start | bytes 524288 | tf_op jit(solution)/shard_map/all_to_all | solution.py:135
  15.3 0.0 copy-done.8
  15.3 4.4 %within.1.a_ref = f32[512,1024]{1,0:T(8,128)} custom-call(bf16[512,1024]{1,0:T(8,128)(2,1)} %q_ref.5, bf16[512,1024]{1,0:T(8,128)(2,1)} %k_ref.3, bf16[512,1024]{1,0:T(8,128)(2,1)} %v_ref.1), custom_call_target="tpu_custom_call" | custom-call | tf_op jit(solution)/shard_map/within/pallas_call | solution.py:218
  19.8 0.0 copy-start.2
  19.8 0.0 copy-start.7
  19.8 3.0 %all-to-all-done.x_ref = bf16[32,32,128]{2,1,0:T(8,128)(2,1)S(1)} async-done(((bf16[32,32,128]{2,1,0:T(8,128)(2,1)}), bf16[32,32,128]{2,1,0:T(8,128)(2,1)S(1)}, u32[]{:S(2)}, u32[]{:S(2)}) %all-to-all-start) | async-done | bytes 262176 | tf_op jit(solution)/shard_map/all_to_all | solution.py:135
  22.8 0.0 copy-start.3
  22.8 15.9 %all_to_all.20 = bf16[32,32,128]{2,1,0:T(8,128)(2,1)S(1)} all-to-all(bf16[32,32,128]{2,1,0:T(8,128)(2,1)S(1)} %prefix.1), channel_id=1, replica_groups={{144,152,160,168,176,184,192,200,208,216,224,232,240,248,0,8,16,24,32,4..., dimensions={0} | all-to-all | bytes 524288 | tf_op jit(solution)/shard_map/all_to_all | solution.py:135
  38.7 0.0 copy-start.4
  38.7 0.0 copy-done.2
  38.7 0.0 copy-done.7
  38.7 0.0 copy-done.3
  38.7 0.8 attend.1
  39.5 0.0 copy-done.4
  39.6 0.1 collective-permute-start
  39.7 1.2 %collective-permute-done = f32[8,128]{1,0:T(8,128)S(1)} collective-permute-done((f32[8,128]{1,0:T(8,128)S(1)}, f32[8,128]{1,0:T(8,128)S(1)}, u32[]{:S(2)}, u32[]{:S(2)}) %collective-permute-start) | collective-permute-done | bytes 4128 | tf_op jit(solution)/shard_map/ppermute | solution.py:140
  40.8 3.0 %collective-permute-start.3 = (f32[8,128]{1,0:T(8,128)S(1)}, f32[8,128]{1,0:T(8,128)S(1)}, u32[]{:S(2)}, u32[]{:S(2)}) collective-permute-start(f32[8,128]{1,0:T(8,128)S(1)} %add.3.s0_ref), channel_id=1, source_target_pairs={{0,6},{1,7},{2,0},{3,1},{4,2},{5,3},{6,4},{7,5},{8,14},{9,15},{10,... | collective-permute-start | bytes 12296 | tf_op jit(solution)/shard_map/ppermute | solution.py:142
  43.8 0.6 collective-permute-start.2
  44.5 1.0 %collective-permute-start.1 = (f32[8,128]{1,0:T(8,128)S(1)}, f32[8,128]{1,0:T(8,128)S(1)}, u32[]{:S(2)}, u32[]{:S(2)}) collective-permute-start(f32[8,128]{1,0:T(8,128)S(1)} %add.3.s0_ref), channel_id=1, source_target_pairs={{0,2},{1,3},{2,4},{3,5},{4,6},{5,7},{6,0},{7,1},{8,10},{9,11},{10,... | collective-permute-start | bytes 12296 | tf_op jit(solution)/shard_map/ppermute | solution.py:142
  45.4 0.0 collective-permute-done.3.s3_ref
  45.4 3.5 %collective-permute-done.2.s2_ref = f32[8,128]{1,0:T(8,128)S(1)} collective-permute-done((f32[8,128]{1,0:T(8,128)S(1)}, f32[8,128]{1,0:T(8,128)S(1)}, u32[]{:S(2)}, u32[]{:S(2)}) %collective-permute-start.2) | collective-permute-done | bytes 4128 | tf_op jit(solution)/shard_map/ppermute | solution.py:142
  48.9 0.3 collective-permute-done.1.s1_ref
  49.3 0.0 copy-start
  49.3 2.0 %grad.1 = (bf16[512,1024]{1,0:T(8,128)(2,1)}, bf16[1024,128]{1,0:T(8,128)(2,1)}, bf16[512,1024]{1,0:T(8,128)(2,1)}) custom-call(f32[512,1024]{1,0:T(8,128)S(1)} %get-tuple-element.24.att_ref, bf16[512,1024]{1,0:T(8,128)(2,1)S(1)} %copy-done.7, bf16[1,1024]{1,0:T(2,128)(2,1)S(1)} %reshape.24.gain_ref, bf16[512,1024]{1,0:T(8,128)(2,1)S(1)} %copy-done.2, ...), custom_call_target="tpu_custom_call" | custom-call | flops 10000000000 | bytes 33333332 | tf_op jit(solution)/shard_map/grad/pallas_call | solution.py:298
  51.2 9.4 %all-to-all-start.2 = ((bf16[32,32,128]{2,1,0:T(8,128)(2,1)}), bf16[32,32,128]{2,1,0:T(8,128)(2,1)S(1)}, u32[]{:S(2)}, u32[]{:S(2)}) async-start(bf16[32,32,128]{2,1,0:T(8,128)(2,1)} %bitcast.8), calls=%async_computation.2 | async-start | bytes 524288 | tf_op jit(solution)/shard_map/all_to_all | solution.py:135
  60.7 0.0 copy-done
  60.7 6.9 %side.1 = (bf16[512,1024]{1,0:T(8,128)(2,1)}, f32[512,1024]{1,0:T(8,128)}, f32[512,1024]{1,0:T(8,128)}) custom-call(bf16[512,1024]{1,0:T(8,128)(2,1)S(1)} %copy-done.2, bf16[512,1024]{1,0:T(8,128)(2,1)S(1)} %copy-done, bf16[512,1024]{1,0:T(8,128)(2,1)} %v_ref.1, bf16[512,1024]{1,0:T(8,128)(2,1)} %get-tuple-element.28.g_hbm, bf16[1024,128]{1,0:T(8,128)(2,1)} %bitcast.5), custom_call_target="tpu_custom_call" | custom-call | tf_op jit(solution)/shard_map/side/pallas_call | solution.py:347
  67.6 0.0 all-to-all-done.2.x_ref
  67.6 0.0 copy-start.1
  67.7 0.0 copy-start.5
  67.7 0.0 copy-start.6
  67.7 16.1 %all_to_all.21 = bf16[32,32,128]{2,1,0:T(8,128)(2,1)S(1)} all-to-all(bf16[32,32,128]{2,1,0:T(8,128)(2,1)S(1)} %suffix.1), channel_id=1, replica_groups={{144,152,160,168,176,184,192,200,208,216,224,232,240,248,0,8,16,24,32,4..., dimensions={0} | all-to-all | bytes 524288 | tf_op jit(solution)/shard_map/all_to_all | solution.py:135
  83.9 0.0 copy-done.1
  83.9 0.0 copy-done.5
  83.9 0.0 copy-done.6
  83.9 1.7 %last.1 = (bf16[512,1024]{1,0:T(8,128)(2,1)}, bf16[512,1024]{1,0:T(8,128)(2,1)}) custom-call(f32[512,1024]{1,0:T(8,128)S(1)} %copy-done.5, f32[512,1024]{1,0:T(8,128)S(1)} %copy-done.6, bf16[512,1024]{1,0:T(8,128)(2,1)S(1)} %copy-done, bf16[512,1024]{1,0:T(8,128)(2,1)S(1)} %copy-done.1, bf16[1024,128]{1,0:T(8,128)(2,1)S(1)} %bitcast.6), custom_call_target="tpu_custom_call" | custom-call | tf_op jit(solution)/shard_map/last/pallas_call | solution.py:376
  (4 shorter events, 0.1 us)
Async XLA Ops:
  0.6 14.7 %copy-start.8 = (bf16[1024]{0:T(1024)(128)(2,1)S(1)}, bf16[1024]{0:T(1024)(128)(2,1)}, u32[]{:S(2)}) copy-start(bf16[1024]{0:T(1024)(128)(2,1)} %param.8) | copy-start | bytes 6148
  3.2 19.6 %all-to-all-start = ((bf16[32,32,128]{2,1,0:T(8,128)(2,1)}), bf16[32,32,128]{2,1,0:T(8,128)(2,1)S(1)}, u32[]{:S(2)}, u32[]{:S(2)}) async-start(bf16[32,32,128]{2,1,0:T(8,128)(2,1)} %bitcast.7), calls=%async_computation | async-start | bytes 524288 | tf_op jit(solution)/shard_map/all_to_all | solution.py:135
  19.8 18.9 %copy-start.2 = (bf16[512,1024]{1,0:T(8,128)(2,1)S(1)}, bf16[512,1024]{1,0:T(8,128)(2,1)}, u32[]{:S(2)}) copy-start(bf16[512,1024]{1,0:T(8,128)(2,1)} %q_ref.5) | copy-start | bytes 3145732
  19.8 18.9 %copy-start.7 = (bf16[512,1024]{1,0:T(8,128)(2,1)S(1)}, bf16[512,1024]{1,0:T(8,128)(2,1)}, u32[]{:S(2)}) copy-start(bf16[512,1024]{1,0:T(8,128)(2,1)} %cot_ref.3) | copy-start | bytes 3145732
  22.8 15.9 %copy-start.3 = (f32[512,1024]{1,0:T(8,128)S(1)}, f32[512,1024]{1,0:T(8,128)}, u32[]{:S(2)}) copy-start(f32[512,1024]{1,0:T(8,128)} %within.1.a_ref) | copy-start | bytes 6291460
  38.7 0.8 copy-start.4
  39.6 1.3 %collective-permute-start = (f32[8,128]{1,0:T(8,128)S(1)}, f32[8,128]{1,0:T(8,128)S(1)}, u32[]{:S(2)}, u32[]{:S(2)}) collective-permute-start(f32[8,128]{1,0:T(8,128)S(1)} %get-tuple-element.25), channel_id=1, source_target_pairs={{0,1},{1,0},{2,3},{3,2},{4,5},{5,4},{6,7},{7,6},{8,9},{9,8},{10,11... | collective-permute-start | bytes 12296 | tf_op jit(solution)/shard_map/ppermute | solution.py:140
  40.8 4.6 %collective-permute-start.3 = (f32[8,128]{1,0:T(8,128)S(1)}, f32[8,128]{1,0:T(8,128)S(1)}, u32[]{:S(2)}, u32[]{:S(2)}) collective-permute-start(f32[8,128]{1,0:T(8,128)S(1)} %add.3.s0_ref), channel_id=1, source_target_pairs={{0,6},{1,7},{2,0},{3,1},{4,2},{5,3},{6,4},{7,5},{8,14},{9,15},{10,... | collective-permute-start | bytes 12296 | tf_op jit(solution)/shard_map/ppermute | solution.py:142
  43.8 5.1 %collective-permute-start.2 = (f32[8,128]{1,0:T(8,128)S(1)}, f32[8,128]{1,0:T(8,128)S(1)}, u32[]{:S(2)}, u32[]{:S(2)}) collective-permute-start(f32[8,128]{1,0:T(8,128)S(1)} %add.3.s0_ref), channel_id=1, source_target_pairs={{0,4},{1,5},{2,6},{3,7},{4,0},{5,1},{6,2},{7,3},{8,12},{9,13},{10,... | collective-permute-start | bytes 12296 | tf_op jit(solution)/shard_map/ppermute | solution.py:142
  44.5 4.8 %collective-permute-start.1 = (f32[8,128]{1,0:T(8,128)S(1)}, f32[8,128]{1,0:T(8,128)S(1)}, u32[]{:S(2)}, u32[]{:S(2)}) collective-permute-start(f32[8,128]{1,0:T(8,128)S(1)} %add.3.s0_ref), channel_id=1, source_target_pairs={{0,2},{1,3},{2,4},{3,5},{4,6},{5,7},{6,0},{7,1},{8,10},{9,11},{10,... | collective-permute-start | bytes 12296 | tf_op jit(solution)/shard_map/ppermute | solution.py:142
  49.3 11.4 %copy-start = (bf16[512,1024]{1,0:T(8,128)(2,1)S(1)}, bf16[512,1024]{1,0:T(8,128)(2,1)}, u32[]{:S(2)}) copy-start(bf16[512,1024]{1,0:T(8,128)(2,1)} %k_ref.3) | copy-start | bytes 3145732
  51.2 16.4 %all-to-all-start.2 = ((bf16[32,32,128]{2,1,0:T(8,128)(2,1)}), bf16[32,32,128]{2,1,0:T(8,128)(2,1)S(1)}, u32[]{:S(2)}, u32[]{:S(2)}) async-start(bf16[32,32,128]{2,1,0:T(8,128)(2,1)} %bitcast.8), calls=%async_computation.2 | async-start | bytes 524288 | tf_op jit(solution)/shard_map/all_to_all | solution.py:135
  67.6 16.2 %copy-start.1 = (bf16[512,1024]{1,0:T(8,128)(2,1)S(1)}, bf16[512,1024]{1,0:T(8,128)(2,1)}, u32[]{:S(2)}) copy-start(bf16[512,1024]{1,0:T(8,128)(2,1)} %v_ref.1) | copy-start | bytes 3145732
  67.7 16.2 %copy-start.5 = (f32[512,1024]{1,0:T(8,128)S(1)}, f32[512,1024]{1,0:T(8,128)}, u32[]{:S(2)}) copy-start(f32[512,1024]{1,0:T(8,128)} %get-tuple-element.33.gk_ref) | copy-start | bytes 6291460
  67.7 16.2 %copy-start.6 = (f32[512,1024]{1,0:T(8,128)S(1)}, f32[512,1024]{1,0:T(8,128)}, u32[]{:S(2)}) copy-start(f32[512,1024]{1,0:T(8,128)} %get-tuple-element.34.gv_ref) | copy-start | bytes 6291460

commit v6 on v5

--- a/solution.py
+++ b/solution.py
@@ -12,6 +12,7 @@
 BF16 = jnp.bfloat16
 PART = F32
 FIRST = 18
+NORM_FIRST = 5
 SCAN_COST = 10_000_000_000
 VMEM_LIMIT = 16 * 1024 * 1024
 VMEM_MOST = 60 * 1024 * 1024
@@ -136,10 +137,7 @@
 
 
 def gathered(x, axis):
-    count = lax.axis_size(axis)
-    pair = x + lax.ppermute(x, axis, [(i, i ^ 1) for i in range(count)])
-    steps = range(2, count, 2)
-    return [pair, *(lax.ppermute(pair, axis, [(i, (i + d) % count) for i in range(count)]) for d in steps)]
+    return lax.all_to_all(x, axis, 0, 0, axis_index_groups=[ring(x.shape[0], NORM_FIRST)])
 
 
 def keep_lower(x):
@@ -247,16 +245,18 @@
             ref[...] = term if i == 0 else ref[...] + term
     chunks = chunks_of(q_ref, DH)
     lines = [jnp.sum(ref[span, :].T, axis=0, keepdims=True) for ref in (sq_ref, cr_ref) for span in chunks]
-    stat_ref[...] = jnp.concatenate(lines, axis=0)
-
-
-def attend(a, q, s, cot, gain):
+    lines = jnp.concatenate(lines, axis=0)
+    for copy in range(stat_ref.shape[0]):
+        stat_ref[copy] = lines
+
+
+def attend(a, q, s, cot, gain, copies):
     rows, width = q.shape
     return pl.pallas_call(
         attend_kernel,
         out_shape=[
             jax.ShapeDtypeStruct((rows, width), F32),
-            jax.ShapeDtypeStruct((2 * rows // DH, DH), F32),
+            jax.ShapeDtypeStruct((copies, 2 * rows // DH, DH), F32),
         ],
         scratch_shapes=[pltpu.VMEM((rows, DH), F32)] * 2,
         compiler_params=params(),
@@ -265,12 +265,12 @@
 
 
 def grad_kernel(
-    att_ref, cot_ref, gain_ref, q_ref, s0_ref, s1_ref, s2_ref, s3_ref, g_hbm, lg_hbm, n_hbm, g_ref, lg_ref, n_ref, sems, *, total
+    att_ref, cot_ref, gain_ref, q_ref, stat_ref, g_hbm, lg_hbm, n_hbm, g_ref, lg_ref, n_ref, sems, *, total
 ):
     mover = Mover(sems)
     rows = att_ref.shape[0]
     blocks = rows // DH
-    stats = ((s0_ref[...] + s1_ref[...]) + (s2_ref[...] + s3_ref[...])) / total
+    stats = jnp.sum(stat_ref[...], axis=0) / total
     inv = lax.rsqrt(stats[:blocks] + 1e-06)
     pull = inv**3 * stats[blocks:]
     stores = []
@@ -283,8 +283,10 @@
             scaled = cot_ref[span, cols].astype(F32) * gain
             g_ref[span, cols] = (inv_tile * scaled - att * pull_tile).astype(BF16)
             n_ref[span, cols] = (att * inv_tile * gain).astype(BF16)
-        stores.append(mover.start(g_ref.at[span], g_hbm.at[span]))
-        stores.append(mover.start(n_ref.at[span], n_hbm.at[span]))
+        if (i + 1) % 2 == 0:
+            rows = slice(span.stop - 2 * DH, span.stop)
+            stores.append(mover.start(g_ref.at[rows], g_hbm.at[rows]))
+            stores.append(mover.start(n_ref.at[rows], n_hbm.at[rows]))
     for cols in heads_of(q_ref):
         lg_ref[cols, :] = dot(q_ref[:, cols], g_ref[:, cols], TN).astype(BF16)
     stores.append(mover.start(lg_ref, lg_hbm))
@@ -304,7 +306,7 @@
         cost_estimate=pl.CostEstimate(flops=SCAN_COST, bytes_accessed=SCAN_COST // 300, transcendentals=0),
         compiler_params=params(),
         name="grad",
-    )(att, cot, gain, q, *stats)
+    )(att, cot, gain, q, stats)
 
 
 def side_kernel(q_ref, k_ref, v_hbm, g_hbm, s_hbm, *refs, sizes):
@@ -394,7 +396,7 @@
     local, a, gain = lax.optimization_barrier((local, a, gain))
     state = exchange(scan(local, False), "ctx").reshape(width, DH)
 
-    att, stats = attend(a, queries, state, cotangent, gain)
+    att, stats = attend(a, queries, state, cotangent, gain, heads)
     stats = gathered(stats, "head")
     g, local, normed = grad(att, cotangent, gain, stats, queries, width * heads)
 

time: 86.1 us -> 85.6 us (level)
  blocking collectives: 32 us -> 39.8 us
  starting transfers between devices: 26.3 us -> 21.6 us
  waiting for transfers between devices: 8 us -> 4.01 us
    all_to_all x0 -> x1, blocking collectives: none -> 7.67 us  [gathered(): lax.all_to_all(x, axis, 0, 0, axis_index_groups=[ring(x.shape[0], NORM_FI...]
    ppermute x4 -> x0, waiting for transfers between devices: 5 us -> none  [the longest x3 3.85 us: gathered(): lax.ppermute(pair, axis, [(i, (i + d) % count) for i in range(count)])]
    ppermute x4 -> x0, starting transfers between devices: 4.71 us -> none  [the longest x3 4.61 us: gathered(): lax.ppermute(pair, axis, [(i, (i + d) % count) for i in range(count)])]
    all_to_all x2, waiting for transfers between devices: 3 us -> 4.01 us  [exchange(): lax.all_to_all(x, axis, 0, 0, axis_index_groups=[ring(x.shape[0], FIRST)])]
  transfers between devices with their start and end apart: 6 -> 2, of which waited for: 4 -> 2; matrix products, arithmetic and copies ran while one was open for 0% -> 0% of each run, Pallas kernels for 13% -> 13%
where the time goes in v6:
time: 85.6 us; the launch traced here: 84.6 us
  blocking collectives  39.8 us (46%)
  starting transfers between devices  21.6 us (25%)
  Pallas kernels  18.4 us (21%)
  waiting for transfers between devices  4.01 us (5%)
    all_to_all x2, blocking collectives, exchange(): lax.all_to_all(x, axis, 0, 0, axis_index_groups=[ring(x.shape[0], FIRST)])  32.1 us
    all_to_all x2, starting transfers between devices, exchange(): lax.all_to_all(x, axis, 0, 0, axis_index_groups=[ring(x.shape[0], FIRST)])  21.6 us
    all_to_all x1, blocking collectives, gathered(): lax.all_to_all(x, axis, 0, 0, axis_index_groups=[ring(x.shape[0], NORM_FI...  7.67 us
    pallas_call x1, Pallas kernels, side(): pl.pallas_call(functools.partial(side_kernel, sizes=sizes), in_specs=[VME...  6.91 us
    pallas_call x1, Pallas kernels, within(): pl.pallas_call(functools.partial(within_kernel, step=step), in_specs=[HBM...  4.43 us
    all_to_all x2, waiting for transfers between devices, exchange(): lax.all_to_all(x, axis, 0, 0, axis_index_groups=[ring(x.shape[0], FIRST)])  4.01 us
    pallas_call x1, Pallas kernels, outer(): pl.pallas_call(functools.partial(outer_kernel, step=step), in_specs=[HBM]...  2.51 us
    pallas_call x1, Pallas kernels, grad(): pl.pallas_call(functools.partial(grad_kernel, total=total), out_specs=[HB...  1.95 us
  transfers between devices with their start and end apart: 2, of which 2 were waited for; matrix products, arithmetic and copies ran while one was open for 0% of the time, Pallas kernels for 13%

profile of v6, /device:TPU:2, one launch (start us, length us, event | category | flops | bytes accessed | tf_op | source)
XLA Modules:
  0.0 84.6 jit_solution(2274970495443025990)
XLA Ops:
  0.6 0.0 copy-start.8
  0.6 2.5 %outer.1 = bf16[1024,128]{1,0:T(8,128)(2,1)} custom-call(bf16[512,1024]{1,0:T(8,128)(2,1)} %k_ref.3, bf16[512,1024]{1,0:T(8,128)(2,1)} %v_ref.1), custom_call_target="tpu_custom_call" | custom-call | tf_op jit(solution)/shard_map/outer/pallas_call | solution.py:94
  3.2 12.1 %all-to-all-start = ((bf16[32,32,128]{2,1,0:T(8,128)(2,1)}), bf16[32,32,128]{2,1,0:T(8,128)(2,1)S(1)}, u32[]{:S(2)}, u32[]{:S(2)}) async-start(bf16[32,32,128]{2,1,0:T(8,128)(2,1)} %bitcast.7), calls=%async_computation | async-start | bytes 524288 | tf_op jit(solution)/shard_map/all_to_all | solution.py:136
  15.3 0.0 copy-done.8
  15.3 4.4 %within.1.a_ref = f32[512,1024]{1,0:T(8,128)} custom-call(bf16[512,1024]{1,0:T(8,128)(2,1)} %q_ref.5, bf16[512,1024]{1,0:T(8,128)(2,1)} %k_ref.3, bf16[512,1024]{1,0:T(8,128)(2,1)} %v_ref.1), custom_call_target="tpu_custom_call" | custom-call | tf_op jit(solution)/shard_map/within/pallas_call | solution.py:216
  19.8 0.0 copy-start.2
  19.8 0.0 copy-start.7
  19.8 3.0 %all-to-all-done.x_ref = bf16[32,32,128]{2,1,0:T(8,128)(2,1)S(1)} async-done(((bf16[32,32,128]{2,1,0:T(8,128)(2,1)}), bf16[32,32,128]{2,1,0:T(8,128)(2,1)S(1)}, u32[]{:S(2)}, u32[]{:S(2)}) %all-to-all-start) | async-done | bytes 262176 | tf_op jit(solution)/shard_map/all_to_all | solution.py:136
  22.8 0.0 copy-start.3
  22.8 15.9 %all_to_all.25 = bf16[32,32,128]{2,1,0:T(8,128)(2,1)S(1)} all-to-all(bf16[32,32,128]{2,1,0:T(8,128)(2,1)S(1)} %prefix.1), channel_id=1, replica_groups={{144,152,160,168,176,184,192,200,208,216,224,232,240,248,0,8,16,24,32,4..., dimensions={0} | all-to-all | bytes 524288 | tf_op jit(solution)/shard_map/all_to_all | solution.py:136
  38.7 0.0 copy-start.4
  38.7 0.0 copy-done.2
  38.7 0.0 copy-done.7
  38.7 0.0 copy-done.3
  38.7 0.8 attend.1
  39.5 0.0 copy-done.4
  39.5 7.7 %all_to_all.26.stat_ref = f32[8,8,128]{2,1,0:T(8,128)S(1)} all-to-all(f32[8,8,128]{2,1,0:T(8,128)S(1)} %get-tuple-element.25), channel_id=1, replica_groups={{5,6,7,0,1,2,3,4},{13,14,15,8,9,10,11,12},{21,22,23,16,17,18,19,20},{29..., dimensions={0} | all-to-all | bytes 65536 | tf_op jit(solution)/shard_map/all_to_all | solution.py:140
  47.2 0.0 copy-start
  47.2 1.9 %grad.1 = (bf16[512,1024]{1,0:T(8,128)(2,1)}, bf16[1024,128]{1,0:T(8,128)(2,1)}, bf16[512,1024]{1,0:T(8,128)(2,1)}) custom-call(f32[512,1024]{1,0:T(8,128)S(1)} %get-tuple-element.24.att_ref, bf16[512,1024]{1,0:T(8,128)(2,1)S(1)} %copy-done.7, bf16[1,1024]{1,0:T(2,128)(2,1)S(1)} %reshape.24.gain_ref, bf16[512,1024]{1,0:T(8,128)(2,1)S(1)} %copy-done.2, ...), custom_call_target="tpu_custom_call" | custom-call | flops 10000000000 | bytes 33333332 | tf_op jit(solution)/shard_map/grad/pallas_call | solution.py:300
  49.1 9.4 %all-to-all-start.3 = ((bf16[32,32,128]{2,1,0:T(8,128)(2,1)}), bf16[32,32,128]{2,1,0:T(8,128)(2,1)S(1)}, u32[]{:S(2)}, u32[]{:S(2)}) async-start(bf16[32,32,128]{2,1,0:T(8,128)(2,1)} %bitcast.8), calls=%async_computation.3 | async-start | bytes 524288 | tf_op jit(solution)/shard_map/all_to_all | solution.py:136
  58.6 0.0 copy-done
  58.6 6.9 %side.1 = (bf16[512,1024]{1,0:T(8,128)(2,1)}, f32[512,1024]{1,0:T(8,128)}, f32[512,1024]{1,0:T(8,128)}) custom-call(bf16[512,1024]{1,0:T(8,128)(2,1)S(1)} %copy-done.2, bf16[512,1024]{1,0:T(8,128)(2,1)S(1)} %copy-done, bf16[512,1024]{1,0:T(8,128)(2,1)} %v_ref.1, bf16[512,1024]{1,0:T(8,128)(2,1)} %get-tuple-element.28.g_hbm, bf16[1024,128]{1,0:T(8,128)(2,1)} %bitcast.5), custom_call_target="tpu_custom_call" | custom-call | tf_op jit(solution)/shard_map/side/pallas_call | solution.py:349
  65.5 1.0 %all-to-all-done.3.x_ref = bf16[32,32,128]{2,1,0:T(8,128)(2,1)S(1)} async-done(((bf16[32,32,128]{2,1,0:T(8,128)(2,1)}), bf16[32,32,128]{2,1,0:T(8,128)(2,1)S(1)}, u32[]{:S(2)}, u32[]{:S(2)}) %all-to-all-start.3) | async-done | bytes 262176 | tf_op jit(solution)/shard_map/all_to_all | solution.py:136
  66.5 0.0 copy-start.1
  66.5 0.0 copy-start.5
  66.5 0.0 copy-start.6
  66.6 16.3 %all_to_all.27 = bf16[32,32,128]{2,1,0:T(8,128)(2,1)S(1)} all-to-all(bf16[32,32,128]{2,1,0:T(8,128)(2,1)S(1)} %suffix.1), channel_id=1, replica_groups={{144,152,160,168,176,184,192,200,208,216,224,232,240,248,0,8,16,24,32,4..., dimensions={0} | all-to-all | bytes 524288 | tf_op jit(solution)/shard_map/all_to_all | solution.py:136
  82.9 0.0 copy-done.1
  82.9 0.0 copy-done.5
  82.9 0.0 copy-done.6
  82.9 1.7 %last.1 = (bf16[512,1024]{1,0:T(8,128)(2,1)}, bf16[512,1024]{1,0:T(8,128)(2,1)}) custom-call(f32[512,1024]{1,0:T(8,128)S(1)} %copy-done.5, f32[512,1024]{1,0:T(8,128)S(1)} %copy-done.6, bf16[512,1024]{1,0:T(8,128)(2,1)S(1)} %copy-done, bf16[512,1024]{1,0:T(8,128)(2,1)S(1)} %copy-done.1, bf16[1024,128]{1,0:T(8,128)(2,1)S(1)} %bitcast.6), custom_call_target="tpu_custom_call" | custom-call | tf_op jit(solution)/shard_map/last/pallas_call | solution.py:378
  (3 shorter events, 0.1 us)
Async XLA Ops:
  0.6 14.7 %copy-start.8 = (bf16[1024]{0:T(1024)(128)(2,1)S(1)}, bf16[1024]{0:T(1024)(128)(2,1)}, u32[]{:S(2)}) copy-start(bf16[1024]{0:T(1024)(128)(2,1)} %param.8) | copy-start | bytes 6148
  3.2 19.6 %all-to-all-start = ((bf16[32,32,128]{2,1,0:T(8,128)(2,1)}), bf16[32,32,128]{2,1,0:T(8,128)(2,1)S(1)}, u32[]{:S(2)}, u32[]{:S(2)}) async-start(bf16[32,32,128]{2,1,0:T(8,128)(2,1)} %bitcast.7), calls=%async_computation | async-start | bytes 524288 | tf_op jit(solution)/shard_map/all_to_all | solution.py:136
  19.8 19.0 %copy-start.2 = (bf16[512,1024]{1,0:T(8,128)(2,1)S(1)}, bf16[512,1024]{1,0:T(8,128)(2,1)}, u32[]{:S(2)}) copy-start(bf16[512,1024]{1,0:T(8,128)(2,1)} %q_ref.5) | copy-start | bytes 3145732
  19.8 18.9 %copy-start.7 = (bf16[512,1024]{1,0:T(8,128)(2,1)S(1)}, bf16[512,1024]{1,0:T(8,128)(2,1)}, u32[]{:S(2)}) copy-start(bf16[512,1024]{1,0:T(8,128)(2,1)} %cot_ref.3) | copy-start | bytes 3145732
  22.8 15.9 %copy-start.3 = (f32[512,1024]{1,0:T(8,128)S(1)}, f32[512,1024]{1,0:T(8,128)}, u32[]{:S(2)}) copy-start(f32[512,1024]{1,0:T(8,128)} %within.1.a_ref) | copy-start | bytes 6291460
  38.7 0.8 copy-start.4
  47.2 11.4 %copy-start = (bf16[512,1024]{1,0:T(8,128)(2,1)S(1)}, bf16[512,1024]{1,0:T(8,128)(2,1)}, u32[]{:S(2)}) copy-start(bf16[512,1024]{1,0:T(8,128)(2,1)} %k_ref.3) | copy-start | bytes 3145732
  49.1 17.4 %all-to-all-start.3 = ((bf16[32,32,128]{2,1,0:T(8,128)(2,1)}), bf16[32,32,128]{2,1,0:T(8,128)(2,1)S(1)}, u32[]{:S(2)}, u32[]{:S(2)}) async-start(bf16[32,32,128]{2,1,0:T(8,128)(2,1)} %bitcast.8), calls=%async_computation.3 | async-start | bytes 524288 | tf_op jit(solution)/shard_map/all_to_all | solution.py:136
  66.5 16.3 %copy-start.1 = (bf16[512,1024]{1,0:T(8,128)(2,1)S(1)}, bf16[512,1024]{1,0:T(8,128)(2,1)}, u32[]{:S(2)}) copy-start(bf16[512,1024]{1,0:T(8,128)(2,1)} %v_ref.1) | copy-start | bytes 3145732
  66.5 16.3 %copy-start.5 = (f32[512,1024]{1,0:T(8,128)S(1)}, f32[512,1024]{1,0:T(8,128)}, u32[]{:S(2)}) copy-start(f32[512,1024]{1,0:T(8,128)} %get-tuple-element.33.gk_ref) | copy-start | bytes 6291460
  66.5 16.3 %copy-start.6 = (f32[512,1024]{1,0:T(8,128)S(1)}, f32[512,1024]{1,0:T(8,128)}, u32[]{:S(2)}) copy-start(f32[512,1024]{1,0:T(8,128)} %get-tuple-element.34.gv_ref) | copy-start | bytes 6291460

commit v7 on v6

--- a/solution.py
+++ b/solution.py
@@ -12,6 +12,7 @@
 BF16 = jnp.bfloat16
 PART = F32
 FIRST = 18
+LATER_FIRST = 19
 NORM_FIRST = 5
 SCAN_COST = 10_000_000_000
 VMEM_LIMIT = 16 * 1024 * 1024
@@ -115,7 +116,7 @@
 def scan_kernel(x_ref, out_ref, *, backward):
     count = x_ref.shape[0]
     total = jnp.zeros(x_ref.shape[1:], F32)
-    place = {block: i for i, block in enumerate(ring(count, FIRST))}
+    place = {block: i for i, block in enumerate(ring(count, LATER_FIRST if backward else FIRST))}
     for lap in range(count):
         i = place[count - 1 - lap if backward else lap]
         out_ref[i] = total.astype(BF16)
@@ -132,8 +133,8 @@
     )(x)
 
 
-def exchange(x, axis):
-    return lax.all_to_all(x, axis, 0, 0, axis_index_groups=[ring(x.shape[0], FIRST)])
+def exchange(x, axis, first):
+    return lax.all_to_all(x, axis, 0, 0, axis_index_groups=[ring(x.shape[0], first)])
 
 
 def gathered(x, axis):
@@ -391,19 +392,19 @@
     gain = gain.reshape(1, width)
     parts = (count, width // count, DH)
 
-    local = exchange(outer(keys, values, 128).reshape(parts), "ctx")
+    local = exchange(outer(keys, values, 128).reshape(parts), "ctx", FIRST)
     a = within(queries, keys, values, 256)
     local, a, gain = lax.optimization_barrier((local, a, gain))
-    state = exchange(scan(local, False), "ctx").reshape(width, DH)
+    state = exchange(scan(local, False), "ctx", FIRST).reshape(width, DH)
 
     att, stats = attend(a, queries, state, cotangent, gain, heads)
     stats = gathered(stats, "head")
     g, local, normed = grad(att, cotangent, gain, stats, queries, width * heads)
 
-    local = exchange(local.reshape(parts), "ctx")
+    local = exchange(local.reshape(parts), "ctx", LATER_FIRST)
     sides = side(queries, keys, values, g, state, (2, 4, 2))
     local, grad_q, gk, gv = lax.optimization_barrier((local, *sides))
-    later = exchange(scan(local, True), "ctx").reshape(width, DH)
+    later = exchange(scan(local, True), "ctx", LATER_FIRST).reshape(width, DH)
     grad_k, grad_v = last(gk, gv, keys, values, later, 256)
     return normed, grad_q, grad_k, grad_v
 

time: 85.6 us -> 85.1 us (level)
  waiting for transfers between devices: 4.01 us -> 3.01 us
    all_to_all x2, waiting for transfers between devices: 4.01 us -> 3.01 us  [exchange(): lax.all_to_all(x, axis, 0, 0, axis_index_groups=[ring(x.shape[0], first)])]
  transfers between devices with their start and end apart: 2 -> 2, of which waited for: 2 -> 1; matrix products, arithmetic and copies ran while one was open for 0% -> 0% of each run, Pallas kernels for 13% -> 13%
where the time goes in v7:
time: 85.1 us; the launch traced here: 84.1 us
  blocking collectives  39.7 us (47%)
  starting transfers between devices  22.2 us (26%)
  Pallas kernels  18.4 us (22%)
  waiting for transfers between devices  3.01 us (4%)
    all_to_all x2, blocking collectives, exchange(): lax.all_to_all(x, axis, 0, 0, axis_index_groups=[ring(x.shape[0], first)])  32 us
    all_to_all x2, starting transfers between devices, exchange(): lax.all_to_all(x, axis, 0, 0, axis_index_groups=[ring(x.shape[0], first)])  22.2 us
    all_to_all x1, blocking collectives, gathered(): lax.all_to_all(x, axis, 0, 0, axis_index_groups=[ring(x.shape[0], NORM_FI...  7.67 us
    pallas_call x1, Pallas kernels, side(): pl.pallas_call(functools.partial(side_kernel, sizes=sizes), in_specs=[VME...  6.91 us
    pallas_call x1, Pallas kernels, within(): pl.pallas_call(functools.partial(within_kernel, step=step), in_specs=[HBM...  4.43 us
    all_to_all x2, waiting for transfers between devices, exchange(): lax.all_to_all(x, axis, 0, 0, axis_index_groups=[ring(x.shape[0], first)])  3.01 us
    pallas_call x1, Pallas kernels, outer(): pl.pallas_call(functools.partial(outer_kernel, step=step), in_specs=[HBM]...  2.51 us
    pallas_call x1, Pallas kernels, grad(): pl.pallas_call(functools.partial(grad_kernel, total=total), out_specs=[HB...  1.95 us
  transfers between devices with their start and end apart: 2, of which 1 were waited for; matrix products, arithmetic and copies ran while one was open for 0% of the time, Pallas kernels for 13%

profile of v7, /device:TPU:2, one launch (start us, length us, event | category | flops | bytes accessed | tf_op | source)
XLA Modules:
  0.0 84.1 jit_solution(4630463310358966590)
XLA Ops:
  0.6 0.0 copy-start.8
  0.6 2.5 %outer.1 = bf16[1024,128]{1,0:T(8,128)(2,1)} custom-call(bf16[512,1024]{1,0:T(8,128)(2,1)} %k_ref.3, bf16[512,1024]{1,0:T(8,128)(2,1)} %v_ref.1), custom_call_target="tpu_custom_call" | custom-call | tf_op jit(solution)/shard_map/outer/pallas_call | solution.py:95
  3.2 12.1 %all-to-all-start = ((bf16[32,32,128]{2,1,0:T(8,128)(2,1)}), bf16[32,32,128]{2,1,0:T(8,128)(2,1)S(1)}, u32[]{:S(2)}, u32[]{:S(2)}) async-start(bf16[32,32,128]{2,1,0:T(8,128)(2,1)} %bitcast.7), calls=%async_computation | async-start | bytes 524288 | tf_op jit(solution)/shard_map/all_to_all | solution.py:137
  15.3 0.0 copy-done.8
  15.3 4.4 %within.1.a_ref = f32[512,1024]{1,0:T(8,128)} custom-call(bf16[512,1024]{1,0:T(8,128)(2,1)} %q_ref.5, bf16[512,1024]{1,0:T(8,128)(2,1)} %k_ref.3, bf16[512,1024]{1,0:T(8,128)(2,1)} %v_ref.1), custom_call_target="tpu_custom_call" | custom-call | tf_op jit(solution)/shard_map/within/pallas_call | solution.py:217
  19.8 0.0 copy-start.2
  19.8 0.0 copy-start.7
  19.8 3.0 %all-to-all-done.x_ref = bf16[32,32,128]{2,1,0:T(8,128)(2,1)S(1)} async-done(((bf16[32,32,128]{2,1,0:T(8,128)(2,1)}), bf16[32,32,128]{2,1,0:T(8,128)(2,1)S(1)}, u32[]{:S(2)}, u32[]{:S(2)}) %all-to-all-start) | async-done | bytes 262176 | tf_op jit(solution)/shard_map/all_to_all | solution.py:137
  22.8 0.0 copy-start.3
  22.8 15.9 %all_to_all.25 = bf16[32,32,128]{2,1,0:T(8,128)(2,1)S(1)} all-to-all(bf16[32,32,128]{2,1,0:T(8,128)(2,1)S(1)} %prefix.1), channel_id=1, replica_groups={{144,152,160,168,176,184,192,200,208,216,224,232,240,248,0,8,16,24,32,4..., dimensions={0} | all-to-all | bytes 524288 | tf_op jit(solution)/shard_map/all_to_all | solution.py:137
  38.7 0.0 copy-start.4
  38.7 0.0 copy-done.2
  38.7 0.0 copy-done.7
  38.7 0.0 copy-done.3
  38.7 0.8 attend.1
  39.5 0.0 copy-done.4
  39.5 7.7 %all_to_all.26.stat_ref = f32[8,8,128]{2,1,0:T(8,128)S(1)} all-to-all(f32[8,8,128]{2,1,0:T(8,128)S(1)} %get-tuple-element.25), channel_id=1, replica_groups={{5,6,7,0,1,2,3,4},{13,14,15,8,9,10,11,12},{21,22,23,16,17,18,19,20},{29..., dimensions={0} | all-to-all | bytes 65536 | tf_op jit(solution)/shard_map/all_to_all | solution.py:141
  47.2 0.0 copy-start
  47.2 1.9 %grad.1 = (bf16[512,1024]{1,0:T(8,128)(2,1)}, bf16[1024,128]{1,0:T(8,128)(2,1)}, bf16[512,1024]{1,0:T(8,128)(2,1)}) custom-call(f32[512,1024]{1,0:T(8,128)S(1)} %get-tuple-element.24.att_ref, bf16[512,1024]{1,0:T(8,128)(2,1)S(1)} %copy-done.7, bf16[1,1024]{1,0:T(2,128)(2,1)S(1)} %reshape.24.gain_ref, bf16[512,1024]{1,0:T(8,128)(2,1)S(1)} %copy-done.2, ...), custom_call_target="tpu_custom_call" | custom-call | flops 10000000000 | bytes 33333332 | tf_op jit(solution)/shard_map/grad/pallas_call | solution.py:301
  49.1 10.0 %all-to-all-start.3 = ((bf16[32,32,128]{2,1,0:T(8,128)(2,1)}), bf16[32,32,128]{2,1,0:T(8,128)(2,1)S(1)}, u32[]{:S(2)}, u32[]{:S(2)}) async-start(bf16[32,32,128]{2,1,0:T(8,128)(2,1)} %bitcast.8), calls=%async_computation.3 | async-start | bytes 524288 | tf_op jit(solution)/shard_map/all_to_all | solution.py:137
  59.2 0.0 copy-done
  59.2 6.9 %side.1 = (bf16[512,1024]{1,0:T(8,128)(2,1)}, f32[512,1024]{1,0:T(8,128)}, f32[512,1024]{1,0:T(8,128)}) custom-call(bf16[512,1024]{1,0:T(8,128)(2,1)S(1)} %copy-done.2, bf16[512,1024]{1,0:T(8,128)(2,1)S(1)} %copy-done, bf16[512,1024]{1,0:T(8,128)(2,1)} %v_ref.1, bf16[512,1024]{1,0:T(8,128)(2,1)} %get-tuple-element.28.g_hbm, bf16[1024,128]{1,0:T(8,128)(2,1)} %bitcast.5), custom_call_target="tpu_custom_call" | custom-call | tf_op jit(solution)/shard_map/side/pallas_call | solution.py:350
  66.1 0.0 all-to-all-done.3.x_ref
  66.1 0.0 copy-start.1
  66.2 0.0 copy-start.5
  66.2 0.0 copy-start.6
  66.2 16.1 %all_to_all.27 = bf16[32,32,128]{2,1,0:T(8,128)(2,1)S(1)} all-to-all(bf16[32,32,128]{2,1,0:T(8,128)(2,1)S(1)} %suffix.1), channel_id=1, replica_groups={{152,160,168,176,184,192,200,208,216,224,232,240,248,0,8,16,24,32,40,48..., dimensions={0} | all-to-all | bytes 524288 | tf_op jit(solution)/shard_map/all_to_all | solution.py:137
  82.4 0.0 copy-done.1
  82.4 0.0 copy-done.5
  82.4 0.0 copy-done.6
  82.4 1.7 %last.1 = (bf16[512,1024]{1,0:T(8,128)(2,1)}, bf16[512,1024]{1,0:T(8,128)(2,1)}) custom-call(f32[512,1024]{1,0:T(8,128)S(1)} %copy-done.5, f32[512,1024]{1,0:T(8,128)S(1)} %copy-done.6, bf16[512,1024]{1,0:T(8,128)(2,1)S(1)} %copy-done, bf16[512,1024]{1,0:T(8,128)(2,1)S(1)} %copy-done.1, bf16[1024,128]{1,0:T(8,128)(2,1)S(1)} %bitcast.6), custom_call_target="tpu_custom_call" | custom-call | tf_op jit(solution)/shard_map/last/pallas_call | solution.py:379
  (3 shorter events, 0.1 us)
Async XLA Ops:
  0.6 14.7 %copy-start.8 = (bf16[1024]{0:T(1024)(128)(2,1)S(1)}, bf16[1024]{0:T(1024)(128)(2,1)}, u32[]{:S(2)}) copy-start(bf16[1024]{0:T(1024)(128)(2,1)} %param.8) | copy-start | bytes 6148
  3.2 19.6 %all-to-all-start = ((bf16[32,32,128]{2,1,0:T(8,128)(2,1)}), bf16[32,32,128]{2,1,0:T(8,128)(2,1)S(1)}, u32[]{:S(2)}, u32[]{:S(2)}) async-start(bf16[32,32,128]{2,1,0:T(8,128)(2,1)} %bitcast.7), calls=%async_computation | async-start | bytes 524288 | tf_op jit(solution)/shard_map/all_to_all | solution.py:137
  19.8 19.0 %copy-start.2 = (bf16[512,1024]{1,0:T(8,128)(2,1)S(1)}, bf16[512,1024]{1,0:T(8,128)(2,1)}, u32[]{:S(2)}) copy-start(bf16[512,1024]{1,0:T(8,128)(2,1)} %q_ref.5) | copy-start | bytes 3145732
  19.8 18.9 %copy-start.7 = (bf16[512,1024]{1,0:T(8,128)(2,1)S(1)}, bf16[512,1024]{1,0:T(8,128)(2,1)}, u32[]{:S(2)}) copy-start(bf16[512,1024]{1,0:T(8,128)(2,1)} %cot_ref.3) | copy-start | bytes 3145732
  22.8 15.9 %copy-start.3 = (f32[512,1024]{1,0:T(8,128)S(1)}, f32[512,1024]{1,0:T(8,128)}, u32[]{:S(2)}) copy-start(f32[512,1024]{1,0:T(8,128)} %within.1.a_ref) | copy-start | bytes 6291460
  38.7 0.8 copy-start.4
  47.2 12.0 %copy-start = (bf16[512,1024]{1,0:T(8,128)(2,1)S(1)}, bf16[512,1024]{1,0:T(8,128)(2,1)}, u32[]{:S(2)}) copy-start(bf16[512,1024]{1,0:T(8,128)(2,1)} %k_ref.3) | copy-start | bytes 3145732
  49.1 17.0 %all-to-all-start.3 = ((bf16[32,32,128]{2,1,0:T(8,128)(2,1)}), bf16[32,32,128]{2,1,0:T(8,128)(2,1)S(1)}, u32[]{:S(2)}, u32[]{:S(2)}) async-start(bf16[32,32,128]{2,1,0:T(8,128)(2,1)} %bitcast.8), calls=%async_computation.3 | async-start | bytes 524288 | tf_op jit(solution)/shard_map/all_to_all | solution.py:137
  66.1 16.2 %copy-start.1 = (bf16[512,1024]{1,0:T(8,128)(2,1)S(1)}, bf16[512,1024]{1,0:T(8,128)(2,1)}, u32[]{:S(2)}) copy-start(bf16[512,1024]{1,0:T(8,128)(2,1)} %v_ref.1) | copy-start | bytes 3145732
  66.2 16.2 %copy-start.5 = (f32[512,1024]{1,0:T(8,128)S(1)}, f32[512,1024]{1,0:T(8,128)}, u32[]{:S(2)}) copy-start(f32[512,1024]{1,0:T(8,128)} %get-tuple-element.33.gk_ref) | copy-start | bytes 6291460
  66.2 16.2 %copy-start.6 = (f32[512,1024]{1,0:T(8,128)S(1)}, f32[512,1024]{1,0:T(8,128)}, u32[]{:S(2)}) copy-start(f32[512,1024]{1,0:T(8,128)} %get-tuple-element.34.gv_ref) | copy-start | bytes 6291460
